TPU v7x, 256 devices: a whole 4x4x8 slice. The times are simulated.
256 devices in a mesh: dp: 16 (over z, y_hi), et: 16 (over y_lo, x, core).
Axes of the slice: x: 4, y: 4 (y_hi: 2, y_lo: 2; y = y_hi * 2 + y_lo), z: 8, core: 2. Of those that a mesh axis runs over, the one named last changes fastest.
Arguments:
- tokens: bfloat16 [16, 2048, 3072], P('dp', 'et'), may hold values from -6 to 6
- cotangent: bfloat16 [16, 2048, 3072], P('dp', 'et'), may hold values from -6 to 6
- route_ids: int32 [16, 2048, 2], P('dp', 'et'), may hold values from 0 to 7, as said below
- route_weight: bfloat16 [16, 2048, 2], P('dp', 'et'), may hold values from 0.25 to 1
- segment_ids: int32 [16, 2048], P('dp', 'et'), may hold values from 0 to 7, never falling along the last dimension, each value on 1 to 512 neighbouring positions
- gate_weight: bfloat16 [3072, 8192], P(None, 'et'), may hold values from -0.109375 to 0.109375
- up_weight: bfloat16 [3072, 8192], P(None, 'et'), may hold values from -0.109375 to 0.109375
- down_weight: bfloat16 [3072, 8192], P(None, 'et'), may hold values from -0.0625 to 0.0625
Outputs:
- grad_tokens: bfloat16 [16, 2048, 3072], P('dp', 'et')
- grad_route: float32 [16, 2048], P('dp', 'et')
- grad_gate: float32 [3072, 8192], P('dp', 'et')
- grad_up: float32 [3072, 8192], P('dp', 'et')
- grad_down: float32 [3072, 8192], P('dp', 'et')
Inputs may be any that keep to these rules, and one draw needn't show every extreme that they name: `route_ids`: each token names two different experts. Among the tokens of one device at most 32 and at least one name expert 0; in every draw the tokens of some device name it exactly 32 times.
All inputs are finite; a program needn't handle non-finite values.
Results may differ from a plain program's by a relative error of at most 0.0058.
Values may be sent and summed in bfloat16 or wider, within the bound.
A program may use at most 192 MiB of HBM per device.

v0:
```python
import jax
import jax.numpy as jnp
from jax import lax
from jax.sharding import PartitionSpec as P

SEGS = 8


def silu_pieces(preact):
    sigmoid_val = jax.nn.sigmoid(preact)
    return (preact * sigmoid_val, sigmoid_val * (1.0 + preact * (1.0 - sigmoid_val)))


def contract_rows(left, right):
    return lax.dot_general(
        left, right, (((0,), (0,)), ((), ())), preferred_element_type=jnp.float32
    )


def contract_cols(left, right):
    return lax.dot_general(
        left, right, (((1,), (1,)), ((), ())), preferred_element_type=jnp.float32
    )


def rounded_partial(value):
    return lax.optimization_barrier(value.astype(jnp.bfloat16)).astype(jnp.float32)


def expert_backward(rows_in, rows_cot, slot_prob, gate_weight, up_weight, down_weight):
    gate_pre = jnp.dot(rows_in, gate_weight, preferred_element_type=jnp.float32)
    up_pre = jnp.dot(rows_in, up_weight, preferred_element_type=jnp.float32)
    active, slope_val = silu_pieces(gate_pre)
    hidden = active * up_pre
    backed = jnp.dot(rows_cot, down_weight, preferred_element_type=jnp.float32)
    route_part = jnp.sum(hidden * backed, axis=1)
    scaled_back = slot_prob[:, None] * backed
    grad_gate_rows = (scaled_back * up_pre * slope_val).astype(jnp.bfloat16)
    grad_up_rows = (scaled_back * active).astype(jnp.bfloat16)
    held_rows = (slot_prob[:, None] * hidden).astype(jnp.bfloat16)
    input_grad = contract_cols(grad_gate_rows, gate_weight) + contract_cols(grad_up_rows, up_weight)
    return (route_part, grad_gate_rows, grad_up_rows, held_rows, input_grad)


def pack_index(routed, total_slots):
    slot_pos = jnp.cumsum(routed.astype(jnp.int32)) - 1
    target = jnp.where(routed, slot_pos, total_slots)
    row_index = (
        jnp.zeros((total_slots,), jnp.int32)
        .at[target]
        .set(jnp.arange(routed.shape[0], dtype=jnp.int32), mode="drop")
    )
    live_slot = jnp.arange(total_slots, dtype=jnp.int32) < jnp.sum(routed.astype(jnp.int32))
    return (row_index, live_slot)


def shards(
    tokens, cotangent, route_ids, route_weight, segment_ids, gate_weight, up_weight, down_weight
):
    shard_in = tokens[0]
    shard_cot = cotangent[0]
    shard_ids = route_ids[0]
    shard_weight = route_weight[0]
    shard_seg = segment_ids[0]
    shard_len = shard_in.shape[0]
    width = shard_in.shape[1]
    capacity = shard_len // 4
    hidden_cols = gate_weight.shape[1]
    labels = jnp.arange(SEGS, dtype=jnp.int32)
    member = (shard_seg[:, None] == labels[None, :]).astype(jnp.float32)
    counts = lax.psum(jnp.sum(member, axis=0), "et")
    weight = 1.0 / jnp.sum(member * counts[None, :], axis=1)
    scaled = (shard_cot.astype(jnp.float32) * weight[:, None]).astype(jnp.bfloat16)
    chosen = shard_ids == 0
    route_prob = jnp.sum(jnp.where(chosen, shard_weight.astype(jnp.float32), 0.0), axis=1)
    routed = jnp.any(chosen, axis=1)
    prob_wire = route_prob.astype(jnp.bfloat16)
    local_index, local_live = pack_index(routed, capacity)
    packed_in = jnp.where(local_live[:, None], shard_in[local_index], jnp.zeros((), jnp.bfloat16))
    packed_cot = jnp.where(local_live[:, None], scaled[local_index], jnp.zeros((), jnp.bfloat16))
    packed_prob = jnp.where(local_live, prob_wire[local_index], jnp.zeros((), jnp.bfloat16))
    rows_in, rows_cot, slot_wire = (
        lax.all_gather(packed_in, "et", axis=0, tiled=True),
        lax.all_gather(packed_cot, "et", axis=0, tiled=True),
        lax.all_gather(packed_prob, "et", axis=0, tiled=True),
    )
    slot_prob = slot_wire.astype(jnp.float32)
    route_part, grad_gate_rows, grad_up_rows, held_rows, input_grad = expert_backward(
        rows_in, rows_cot, slot_prob, gate_weight, up_weight, down_weight
    )
    slot_grad, slot_route = (
        lax.psum_scatter(input_grad, "et", scatter_dimension=0, tiled=True),
        lax.psum_scatter(route_part, "et", scatter_dimension=0, tiled=True),
    )
    grad_rows = (
        jnp.zeros((shard_len, width), jnp.float32)
        .at[local_index]
        .add(jnp.where(local_live[:, None], slot_grad, 0.0))
    )
    route_rows = (
        jnp.zeros((shard_len,), jnp.float32)
        .at[local_index]
        .add(jnp.where(local_live, slot_route, 0.0))
    )
    summed = lax.psum_scatter(
        jnp.concatenate(
            [
                rounded_partial(contract_rows(rows_in, grad_gate_rows)),
                rounded_partial(contract_rows(rows_in, grad_up_rows)),
                rounded_partial(contract_rows(rows_cot, held_rows)),
            ],
            axis=1,
        ),
        "dp",
        scatter_dimension=0,
        tiled=True,
    )
    grad_gate = summed[:, :hidden_cols]
    grad_up = summed[:, hidden_cols : 2 * hidden_cols]
    grad_down = summed[:, 2 * hidden_cols :]
    return (grad_rows.astype(jnp.bfloat16)[None], route_rows[None], grad_gate, grad_up, grad_down)


def solution(mesh):
    return jax.shard_map(
        shards,
        mesh=mesh,
        in_specs=(
            P("dp", "et", None),
            P("dp", "et", None),
            P("dp", "et", None),
            P("dp", "et", None),
            P("dp", "et"),
            P(None, "et"),
            P(None, "et"),
            P(None, "et"),
        ),
        out_specs=(P("dp", "et", None), P("dp", "et"), P("dp", "et"), P("dp", "et"), P("dp", "et")),
        check_vma=False,
    )
```

profile of v0, /device:TPU:1, one launch (start us, length us, event | category | flops | bytes accessed | tf_op | source)
XLA Modules:
  0.0 542.7 jit_solution(9172530730004095944)
XLA Ops:
  7.2 0.0 copy-start
  7.2 0.0 all-gather.5.cloned.1.call-start
  7.2 0.8 fusion.14
  8.1 0.6 convert_reduce_fusion.1
  8.7 0.8 convert_reduce_fusion
  9.5 0.7 iota_compare_fusion.1
  10.1 29.7 %psum.7 = f32[8]{0:T(128)S(1)} all-reduce(f32[8]{0:T(128)S(1)} %convert_reduce_fusion), channel_id=1, replica_groups=mesh['dp'=16,'et'=16] {'et'}, use_global_device_ids=true, to_apply=%region_6.7 | all-reduce | flops 8 | bytes 64 | tf_op jit(solution)/shard_map/psum | solution.py:71
  39.9 0.7 select_reduce_fusion
  40.6 0.1 copy.20
  40.8 0.1 copy.19
  40.9 0.2 reduce-window.4
  41.0 0.1 fusion.9
  41.2 1.0 scatter_custom_fusion
  42.2 0.0 copy-start.10
  42.2 0.0 copy-start.9
  42.2 0.0 copy-start.8
  42.2 2.1 gather_fusion.2
  44.3 0.0 copy-done.10
  44.3 2.2 fusion
  46.6 2.1 gather_fusion.1
  48.7 0.8 broadcast_select_fusion.1
  49.5 0.0 all-gather.5.cloned.1.call-update
  49.5 0.0 all-gather.3.cloned.1.call-start
  49.6 0.7 all-gather.3.cloned.1.call-update
  50.3 0.0 reduce-scatter.3.cloned.1.call-start
  50.3 0.0 copy-done.9
  50.4 0.7 select_reduce_fusion.1
  51.0 0.7 gather_fusion
  51.7 0.0 copy-done.8
  51.8 0.6 fusion.17
  53.0 0.7 broadcast_select_fusion.2
  53.7 0.2 dynamic-update-slice
  53.9 29.2 %all-reduce = bf16[512]{0:T(512)(128)(2,1)S(1)} all-reduce(bf16[512]{0:T(512)(128)(2,1)S(1)} %dynamic-update-slice), channel_id=1, replica_groups=mesh['dp'=16,'et'=16] {'et'}, use_global_device_ids=true, to_apply=%add | all-reduce | flops 512 | bytes 2048
  83.1 7.0 %all-gather.5.cloned.1.call-done = bf16[512,3072]{1,0:T(8,128)(2,1)} async-done(((bf16[32,3072]{1,0:T(8,128)(2,1)}), bf16[512,3072]{1,0:T(8,128)(2,1)}) %all-gather.5.cloned.1.call-update) | async-done | bytes 3145744 | tf_op jit(solution)/shard_map/all_gather | solution.py:83
  90.1 0.0 copy-done
  90.1 4.9 fusion.19
  95.0 0.0 copy-done.2
  95.0 2.8 fusion.18
  97.8 33.3 %all-gather.3.cloned.1.call-done = bf16[512,3072]{1,0:T(8,128)(2,1)} async-done(((bf16[32,3072]{1,0:T(8,128)(2,1)}), bf16[512,3072]{1,0:T(8,128)(2,1)}) %all-gather.3.cloned.1.call-update) | async-done | bytes 3145744 | tf_op jit(solution)/shard_map/all_gather | solution.py:84
  131.1 5.6 %multiply_reduce_fusion = (f32[512]{0:T(512)S(1)}, bf16[512,512]{0,1:T(8,128)(2,1)S(1)}, bf16[512,512]{0,1:T(8,128)(2,1)S(1)}) fusion(f32[512,512]{0,1:T(8,128)} %fusion.18, f32[512,512]{0,1:T(8,128)} %fusion.19, f32[512]{0:T(512)S(1)} %convert_element_type.63, bf16[512,3072]{1,0:T(8,128)(2,1)} %all-gather.3.cloned.1.call-done, bf16[3072,512]{1,0:T(8,128)(2,1)} %param.15), kind=kOutput, calls=%fused_computation.14 | convolution fusion | flops 1615068672 | bytes 9441280 | tf_op jit(solution)/shard_map/dot_general | solution.py:35
  136.8 0.0 copy-start.4
  136.8 0.0 copy-start.3
  136.8 1.9 fusion.20
  138.6 0.0 copy-done.6
  138.6 0.0 copy-done.4
  138.7 0.4 copy-done.3
  139.0 4.5 convolution_add_fusion
  143.5 0.0 reduce-scatter.3.cloned.1.call-update
  143.5 0.3 reduce-scatter.5.cloned.1.call-start
  143.8 0.0 copy-start.5
  143.8 4.6 convolution_convert_fusion
  148.4 1.9 convolution_convert_fusion.1
  150.3 1.9 convolution_convert_fusion.2
  152.2 7.2 %maximum_convert_fusion = f32[3072,1536]{1,0:T(8,128)} fusion(bf16[3072,512]{1,0:T(8,128)(2,1)S(1)} %convolution_convert_fusion, bf16[3072,512]{1,0:T(8,128)(2,1)S(1)} %convolution_convert_fusion.1, bf16[3072,512]{1,0:T(8,128)(2,1)S(1)} %convolution_convert_fusion.2), kind=kLoop, calls=%fused_computation.6 | loop fusion | flops 28311552 | bytes 28311552 | tf_op jit(solution)/shard_map/concatenate | solution.py:106
  159.5 0.0 reduce-scatter.5.cloned.1.call-update
  160.1 26.8 %all-reduce.1 = f32[512]{0:T(512)S(1)} all-reduce(f32[512]{0:T(512)S(1)} %get-tuple-element.5), channel_id=3, replica_groups=mesh['dp'=16,'et'=16] {'et'}, use_global_device_ids=true, to_apply=%region_11.12.clone | all-reduce | flops 512 | bytes 4096
  186.9 0.7 dynamic-slice_select_fusion
  187.6 1.5 scatter_custom_fusion.2
  189.2 24.1 %reduce-scatter.3.cloned.1.call-done = f32[32,3072]{1,0:T(8,128)} async-done(((f32[512,3072]{1,0:T(8,128)}), f32[32,3072]{1,0:T(8,128)}) %reduce-scatter.3.cloned.1.call-update) | async-done | bytes 393232 | tf_op jit(solution)/shard_map/reduce_scatter | solution.py:92
  213.3 2.9 scatter_custom_fusion.1
  216.2 2.4 convert_bitcast_fusion
  218.6 315.4 %reduce-scatter.5.cloned.1.call-done = f32[192,1536]{1,0:T(8,128)} async-done(((f32[3072,1536]{1,0:T(8,128)}), f32[192,1536]{1,0:T(8,128)}) %reduce-scatter.5.cloned.1.call-update) | async-done | bytes 1179664 | tf_op jit(solution)/shard_map/reduce_scatter | solution.py:105
  533.9 2.3 fusion.16
  536.2 0.0 copy-done.1
  (17 shorter events, 0.1 us)
Async XLA Ops:
  7.2 83.0 %copy-start = (bf16[3072,512]{1,0:T(8,128)(2,1)S(1)}, bf16[3072,512]{1,0:T(8,128)(2,1)}, u32[]{:S(2)}) copy-start(bf16[3072,512]{1,0:T(8,128)(2,1)} %param.13) | copy-start | bytes 9437188
  7.2 82.9 %all-gather.5.cloned.1.call-start = ((), (), s32[]{:S(2)}) async-start(), calls=%async_computation.3 | async-start | bytes 3342336 | tf_op jit(solution)/shard_map/all_gather | solution.py:83
  42.2 2.2 copy-start.10
  42.2 8.2 %copy-start.9 = (s32[1,128,2]{1,2,0:T(2,128)S(1)}, s32[1,128,2]{1,2,0:T(2,128)}, u32[]{:S(2)}) copy-start(s32[1,128,2]{1,2,0:T(2,128)} %param.10) | copy-start | bytes 3076
  42.2 9.5 %copy-start.8 = (u32[256]{0:T(256)S(1)}, u32[256]{0:T(256)}, u32[]{:S(2)}) copy-start(u32[256]{0:T(256)} %constant.35) | copy-start | bytes 3076
  49.5 81.6 %all-gather.3.cloned.1.call-start = ((), (), s32[]{:S(2)}) async-start(), calls=%async_computation.2 | async-start | bytes 3342336 | tf_op jit(solution)/shard_map/all_gather | solution.py:84
  50.3 163.0 %reduce-scatter.3.cloned.1.call-start = ((), (), s32[]{:S(2)}) async-start(), calls=%async_computation.4 | async-start | bytes 6684672 | tf_op jit(solution)/shard_map/reduce_scatter | solution.py:92
  90.1 4.9 copy-start.2
  90.1 4.9 copy-start.11
  136.7 1.9 copy-start.6
  136.8 1.9 copy-start.4
  136.8 2.3 copy-start.3
  143.5 390.4 %reduce-scatter.5.cloned.1.call-start = ((), (), s32[]{:S(2)}) async-start(), calls=%async_computation.5 | async-start | bytes 20054016 | tf_op jit(solution)/shard_map/reduce_scatter | solution.py:105
  143.8 4.6 copy-start.5
  143.8 4.6 copy-start.12
  148.4 1.9 copy-start.7
  187.6 348.6 %copy-start.1 = (bf16[3072,512]{1,0:T(8,128)(2,1)S(1)}, bf16[3072,512]{1,0:T(8,128)(2,1)}, u32[]{:S(2)}) copy-start(bf16[3072,512]{1,0:T(8,128)(2,1)} %param.13) | copy-start | bytes 9437188
Sparse Core Ops, SparseCore 0:
  49.6 40.4 all-gather.4
  92.5 38.5 all-gather.2
  143.6 69.6 reduce-scatter.2
  217.3 316.5 reduce-scatter.4
where the time goes:
time: 543 us
  waiting for transfers between devices  381 us (70%)
  blocking collectives  85.8 us (16%)
  matrix products  28 us (5%)
  other arithmetic  23.1 us (4%)
  between operations  15.3 us (3%)
  local copies, waits for them, and re-layouts  9.69 us (2%)
    reduce_scatter x1, waiting for transfers between devices, shards(): lax.psum_scatter(jnp.concatenate([rounded_partial(contract_rows(rows_in,...  315 us
    unnamed x2, blocking collectives  56 us
    all_gather x1, waiting for transfers between devices, shards(): lax.all_gather(packed_cot, 'et', axis=0, tiled=True)  33.3 us
    psum x1, blocking collectives, shards(): counts = lax.psum(jnp.sum(member, axis=0), 'et')  29.7 us
    reduce_scatter x1, waiting for transfers between devices, shards(): lax.psum_scatter(input_grad, 'et', scatter_dimension=0, tiled=True)  24.1 us
  transfers between devices with their start and end apart: 4, of which 4 were waited for; matrix products, arithmetic and copies ran while one was open for 6% of the time, Pallas kernels for 0%

commit v1 on v0

v1 whole, which is shorter than its diff:
```python
import jax
import jax.numpy as jnp
from jax import lax
from jax.experimental import pallas as pl
from jax.experimental.pallas import tpu as pltpu
from jax.sharding import PartitionSpec as P

MESH = pl.DeviceIdType.MESH
F32 = jnp.float32
BF16 = jnp.bfloat16
NZ = 8
QW = 768
ZW = 384
FH = 256
SL = 32


def nn(a, b):
    return jnp.dot(a, b, preferred_element_type=F32)


def nt(a, b):
    return lax.dot_general(a, b, (((1,), (1,)), ((), ())), preferred_element_type=F32)


def wrap(v, n):
    return lax.rem(v + 2 * n, n)


def kernel(
    tok_ref, cot_ref, ids_ref, rw_ref, seg_ref, wg_hbm, wu_hbm, wd_hbm,
    gt_ref, gr_ref, gg_ref, gu_ref, gd_ref,
    tb, cb, meta, cnt, wgu, wd, pre, dgu, dT, zs, zr, sgs, sgr, p1s, p1r, p2s, p2r, g2,
    q1s, q1r, q2s, q2r, fin, fing, rps, rpr, fsum, fxs, fxr,
    w_sem, ag_s, ag_r, sib_s, sib_r, m_s, m_r, z_s, z_r, g_s, g_r, rt_s, rt_r, fx_s, fx_r,
):
    dp, et = lax.axis_index("dp"), lax.axis_index("et")
    z, yh = lax.div(dp, 2), lax.rem(dp, 2)
    yl, x, c = lax.div(et, 8), lax.rem(lax.div(et, 2), 4), lax.rem(et, 2)
    y = yh * 2 + yl
    p, r = y + c * (x - y), x + c * (y - x)

    def dev(xx, yy, zz, cc):
        return (zz * 2 + lax.div(yy, 2), lax.rem(yy, 2) * 8 + xx * 2 + cc)

    def at(dp_, dr_):
        pp, rr = wrap(p + dp_, 4), wrap(r + dr_, 4)
        return dev(rr + c * (pp - rr), pp + c * (rr - pp), z, c)

    def pos(dp_, dr_):
        return wrap(p + dp_, 4) * 4 + wrap(r + dr_, 4)

    sib = dev(x, y, z, 1 - c)
    zplus, zminus = dev(x, y, wrap(z + 1, NZ), c), dev(x, y, wrap(z - 1, NZ), c)

    def flip(v, bit):
        return v + bit - 2 * bit * lax.rem(lax.div(v, bit), 2)

    hyper = [sib, dev(flip(x, 1), y, z, c), dev(flip(x, 2), y, z, c),
             dev(x, flip(y, 1), z, c), dev(x, flip(y, 2), z, c)]
    partner = hyper[4]

    half = pl.ds(pl.multiple_of(yh * FH, FH), FH)
    wcopies = [
        pltpu.make_async_copy(wg_hbm.at[:, half], wgu.at[:, pl.ds(0, FH)], w_sem.at[0]),
        pltpu.make_async_copy(wu_hbm.at[:, half], wgu.at[:, pl.ds(FH, FH)], w_sem.at[1]),
        pltpu.make_async_copy(wd_hbm.at[:, half], wd, w_sem.at[2]),
    ]
    for cp in wcopies:
        cp.start()

    barrier = pltpu.get_barrier_semaphore()
    for nb in (sib, at(1, 0), at(-1, 0), at(0, 1), at(0, -1), at(2, 0), at(0, 2), zplus, zminus):
        pl.semaphore_signal(barrier, inc=1, device_id=nb, device_id_type=MESH)

    sent = []

    def copy(src, dst, ss, rs, to):
        return pltpu.make_async_remote_copy(
            src_ref=src, dst_ref=dst, send_sem=ss, recv_sem=rs, device_id=to, device_id_type=MESH)

    def send(src, dst, ss, rs, to):
        cp = copy(src, dst, ss, rs, to)
        cp.start()
        sent.append(cp)

    def arrived(ref, ss, rs):
        copy(ref, ref, ss, rs, sib).wait_recv()

    n = 128
    row_i = lax.broadcasted_iota(jnp.int32, (n, n), 0)
    col_i = lax.broadcasted_iota(jnp.int32, (n, n), 1)
    chosen = ids_ref[...] == 0
    routed = jnp.max(chosen.astype(F32), axis=1, keepdims=True)
    prob = jnp.sum(jnp.where(chosen, rw_ref[...].astype(F32), 0.0), axis=1, keepdims=True)
    routed_c = jnp.broadcast_to(routed, (n, n))
    routed_r = routed_c.T
    before = (row_i < col_i).astype(F32).astype(BF16)
    after = (col_i < row_i).astype(F32).astype(BF16)
    slot_r = nn(routed_r.astype(BF16), before)
    slot_c = nn(after, routed_c.astype(BF16))
    pick = jnp.where((slot_r == row_i.astype(F32)) & (routed_r > 0.5), 1.0, 0.0)[:SL].astype(BF16)
    place = jnp.where((slot_c == col_i.astype(F32)) & (routed_c > 0.5), 1.0, 0.0)[:, :SL].astype(BF16)

    mine = pl.ds(pl.multiple_of(c * SL, SL), SL)
    here = p * 4 + r
    there = r * 4 + p

    def pack(src, buf):
        for h in range(2):
            for q in range(2):
                cols = slice((h * 2 + q) * QW, (h * 2 + q + 1) * QW)
                buf[h, here, q, mine, :] = nn(pick, src[:, cols]).astype(BF16)

    def swap(t, buf):
        for k, h in ((0, 1 - c), (1, c)):
            send(buf.at[h, here, :, mine, :], buf.at[h, there, :, mine, :],
                 sib_s.at[t, 16 + k], sib_r.at[t, 16 + k], sib)

    other = pl.ds(pl.multiple_of((1 - c) * SL, SL), SL)

    def swapped(t, buf, k):
        h = c if k == 0 else 1 - c
        arrived(buf.at[h, here, :, other, :], sib_s.at[t, 16 + k], sib_r.at[t, 16 + k])

    me_idx = (y * 4 + x) * 2 + c
    seg = jnp.broadcast_to(seg_ref[...], (n, n))
    member = jnp.where(seg == row_i, 1.0, 0.0).astype(BF16)
    prob_m = jnp.where(col_i == 16, jnp.broadcast_to(prob, (n, n)), 0.0).astype(BF16)
    meta[me_idx, pl.ds(0, SL), :] = (nt(pick, member) + nn(pick, prob_m)).astype(BF16)
    meta[me_idx, pl.ds(SL, 16), :] = nt(jnp.ones((16, n), BF16), member).astype(BF16)

    pack(tok_ref, tb)
    pl.semaphore_wait(barrier, 9)
    swap(0, tb)

    def meta_send(k):
        size = 1 << k
        base = lax.div(me_idx, size) * size
        ref = meta.at[pl.ds(base, size)]
        send(ref, ref, m_s.at[k], m_r.at[k], hyper[k])

    def meta_got(k):
        size = 1 << k
        base = flip(lax.div(me_idx, size), 1) * size
        arrived(meta.at[pl.ds(base, size)], m_s.at[k], m_r.at[k])

    meta_send(0)
    pack(cot_ref, cb)

    line = (0, -1, 1, 2)

    def ag(t, buf):
        def one(dst_p, dst_r, q, k, to):
            ref = buf.at[c, pos(dst_p, dst_r)] if q is None else buf.at[c, pos(dst_p, dst_r), q]
            send(ref, ref, ag_s.at[t, k], ag_r.at[t, k], to)

        def got(dst_p, dst_r, q, k):
            ref = buf.at[c, pos(dst_p, dst_r)] if q is None else buf.at[c, pos(dst_p, dst_r), q]
            arrived(ref, ag_s.at[t, k], ag_r.at[t, k])

        def to_sib(a, b):
            k = (a % 4) * 4 + b % 4
            send(buf.at[c, pos(a, b)], buf.at[c, wrap(r + b, 4) * 4 + wrap(p + a, 4)],
                 sib_s.at[t, k], sib_r.at[t, k], sib)

        def out_p(j):
            one(0, line[j], None, 4 + 4 * j, at(1, 0))
            one(0, line[j], None, 5 + 4 * j, at(-1, 0))

        def begin():
            one(0, 0, None, 0, at(0, 1))
            one(0, 0, None, 1, at(0, -1))
            out_p(0)

        def first():
            got(0, -1, None, 0)
            one(0, -1, 0, 2, at(0, 1))
            out_p(1)
            to_sib(0, -1)
            got(0, 1, None, 1)
            one(0, 1, 1, 3, at(0, -1))
            out_p(2)
            to_sib(0, 1)

        def second():
            got(0, 2, 0, 2)
            got(0, 2, 1, 3)
            out_p(3)
            to_sib(0, 2)

        def near(j):
            got(-1, line[j], None, 4 + 4 * j)
            one(-1, line[j], 0, 6 + 4 * j, at(1, 0))
            to_sib(-1, line[j])
            got(1, line[j], None, 5 + 4 * j)
            one(1, line[j], 1, 7 + 4 * j, at(-1, 0))
            to_sib(1, line[j])

        def far(j):
            got(2, line[j], 0, 6 + 4 * j)
            got(2, line[j], 1, 7 + 4 * j)
            to_sib(2, line[j])

        def from_sib():
            for a in range(4):
                for b in range(4):
                    if a or b:
                        k = a * 4 + b
                        arrived(buf.at[1 - c, pos(b, a)], sib_s.at[t, k], sib_r.at[t, k])
            swapped(t, buf, 1)

        return begin, first, second, near, far, from_sib

    T, C = ag(0, tb), ag(1, cb)
    swapped(0, tb, 0)
    T[0]()
    swap(1, cb)
    meta_got(0)
    meta_send(1)
    T[1]()
    meta_got(1)
    meta_send(2)
    T[2]()
    swapped(1, cb, 0)
    meta_got(2)
    meta_send(3)
    T[3](0)
    C[0]()
    T[3](1)
    meta_got(3)
    meta_send(4)
    T[4](0)
    T[3](2)
    T[4](1)
    T[3](3)
    T[4](2)
    T[4](3)
    C[1]()
    T[5]()
    C[2]()
    meta_got(4)

    for g in range(2):
        cnt[g] = jnp.sum(meta[pl.ds(16 * g, 16), pl.ds(SL, 16), :].astype(F32), axis=0)[:8]

    for cp in wcopies:
        cp.wait()

    def fwd(i):
        rows = pl.ds(pl.multiple_of(i * 256, 256), 256)
        acc = None
        for h in range(2):
            for q in range(2):
                xs = tb[h, pl.ds(i * 4, 4), q].reshape(256, QW)
                part = nn(xs, wgu[(h * 2 + q) * QW:(h * 2 + q + 1) * QW, :])
                acc = part if acc is None else acc + part
        pre[rows, :] = acc

    C[3](0)
    fwd(0)
    C[3](1)
    C[4](0)
    fwd(1)
    C[3](2)
    C[4](1)
    fwd(2)
    C[3](3)
    C[4](2)
    fwd(3)
    C[4](3)
    C[5]()

    lane = lax.broadcasted_iota(jnp.int32, (n, n), 1)

    @pl.loop(0, 8)
    def _(j):
        rows = pl.ds(pl.multiple_of(j * n, n), n)
        back = None
        for h in range(2):
            for q in range(2):
                xs = cb[h, pl.ds(j * 2, 2), q].reshape(n, QW)
                part = nn(xs, wd[(h * 2 + q) * QW:(h * 2 + q + 1) * QW, :])
                back = part if back is None else back + part
        chips, metas, counts = [], [], []
        for k in range(2):
            i = j * 2 + k
            chip = i + c * (lax.rem(i, 4) * 4 + lax.div(i, 4) - i)
            m = meta[pl.ds(chip * 2, 2), pl.ds(0, SL), :].astype(F32).reshape(2 * SL, n)
            chips.append(chip)
            metas.append(m)
            counts.append(jnp.where(lane[:64] < 8, m * cnt[lax.div(chip, 8)][0:1], 0.0))
        m = jnp.concatenate(metas, axis=0)
        count = jnp.sum(jnp.concatenate(counts, axis=0), axis=1, keepdims=True)
        weight = jnp.where(count > 0.0, 1.0 / jnp.maximum(count, 1.0), 0.0)
        pr = jnp.sum(jnp.where(lane == 16, m, 0.0), axis=1, keepdims=True)
        gate, up = pre[rows, 0:FH], pre[rows, FH:2 * FH]
        back = back * weight
        sg = 1.0 / (1.0 + jnp.exp(-gate))
        act = gate * sg
        slope = sg * (1.0 + gate * (1.0 - sg))
        hid = act * up
        rp = jnp.sum(hid * back, axis=1, keepdims=True)
        sb = back * pr
        dg = sb * up * slope
        du = sb * act
        he = hid * (pr * weight)
        dgu[lax.div(j, 2), lax.rem(j, 2), :, 0:FH] = dg.astype(BF16)
        dgu[lax.div(j, 2), lax.rem(j, 2), :, FH:2 * FH] = du.astype(BF16)
        dT[0:FH, rows] = dg.T.astype(BF16)
        dT[FH:2 * FH, rows] = du.T.astype(BF16)
        dT[2 * FH:3 * FH, rows] = he.T.astype(BF16)
        rp_row = jnp.broadcast_to(rp, (n, n)).T[0:1]
        rps[0, pl.ds(chips[0], 1), :] = jnp.where(lane[0:1] < 64, rp_row, 0.0)
        rps[0, pl.ds(chips[1], 1), :] = jnp.where(lane[0:1] < 64, pltpu.roll(rp_row, 64, 1), 0.0)

    def part(u, d):
        buf = cb if u == 2 else tb
        cols = pl.ds(pl.multiple_of(lax.rem(d, 2) * ZW, 128), ZW)
        xs = buf[lax.div(d, 4), :, lax.rem(lax.div(d, 2), 2), :, cols].reshape(1024, ZW)
        return nn(dT[u * FH:(u + 1) * FH, :], xs)

    units = (2, 0, 1)
    HF = FH // 2
    STEPS = NZ // 2

    def z_unit(s, u):
        if s == 1:
            val = part(u, wrap(z + STEPS, NZ)).astype(BF16)
            for dr, to in ((0, zplus), (1, zminus)):
                zs[dr, 0, u, dr * HF:(dr + 1) * HF, :] = val[dr * HF:(dr + 1) * HF]
                ref = (dr, 0, u, pl.ds(dr * HF, HF))
                send(zs.at[ref], zr.at[ref], z_s.at[dr, 0, u], z_r.at[dr, 0, u], to)
            return
        for dr, to, off in ((0, zplus, STEPS + 1 - s), (1, zminus, s - STEPS - 1)):
            val = part(u, wrap(z + off, NZ))
            if s == 2:
                ref = zr.at[dr, 0, u, pl.ds(dr * HF, HF)]
                arrived(ref, z_s.at[dr, 0, u], z_r.at[dr, 0, u])
                lo, hi = dr * HF, (dr + 1) * HF
                o_lo, o_hi = HF - lo, FH - lo
                zs[dr, 1, u, lo:hi, :] = (val[lo:hi] + ref[...].astype(F32)).astype(BF16)
                zs[dr, 1, u, o_lo:o_hi, :] = val[o_lo:o_hi].astype(BF16)
            else:
                ref = zr.at[dr, s - 2, u]
                arrived(ref, z_s.at[dr, s - 2, u], z_r.at[dr, s - 2, u])
                zs[dr, s - 1, u] = (val + ref[...].astype(F32)).astype(BF16)
            send(zs.at[dr, s - 1, u], zr.at[dr, s - 1, u], z_s.at[dr, s - 1, u], z_r.at[dr, s - 1, u], to)

    def z_step(s):
        for u in units:
            z_unit(s, u)

    outs = (gg_ref, gu_ref, gd_ref)
    mycols = pl.ds(pl.multiple_of(yh * FH, FH), FH)
    yourcols = pl.ds(pl.multiple_of((1 - yh) * FH, FH), FH)

    def z_last(u):
        val = part(u, z)
        for dr in range(2):
            ref = zr.at[dr, STEPS - 1, u]
            arrived(ref, z_s.at[dr, STEPS - 1, u], z_r.at[dr, STEPS - 1, u])
            val = val + ref[...].astype(F32)
        fsum[u] = val.T
        fxs[u] = fsum[u, pl.ds(pl.multiple_of((1 - yh) * 192, 192), 192), :].astype(BF16)
        send(fxs.at[u], fxr.at[u], fx_s.at[u], fx_r.at[u], partner)
        outs[u][:, mycols] = fsum[u, pl.ds(pl.multiple_of(yh * 192, 192), 192), :]

    def z_out(u):
        arrived(fxr.at[u], fx_s.at[u], fx_r.at[u])
        outs[u][:, yourcols] = fxr[u].astype(F32)

    def wrows(h, q):
        return wgu[pl.ds(pl.multiple_of((h * 2 + q) * QW, QW), QW), :]

    def g_sib(k):
        rr = wrap(r + (2, 1, -1, 0)[k], 4)
        j0, odd = lax.div(rr, 2), lax.rem(rr, 2)
        xs = dgu[:, j0, pl.ds(pl.multiple_of(odd * 64, 64), 64), :].reshape(256, 2 * FH)
        for q in range(2):
            sgs[rr, :, q] = nt(xs, wrows(1 - c, q)).astype(BF16).reshape(4, 64, QW)
        send(sgs.at[rr], sgr.at[rr], g_s.at[k], g_r.at[k], sib)

    def g_line(off, k):
        pp = wrap(p + off, 4)
        arrived(sgr.at[pp], g_s.at[k], g_r.at[k])
        xs = dgu[pp].reshape(256, 2 * FH)
        return [nt(xs, wrows(c, q)).reshape(4, 64, QW) + sgr[pp, :, q].astype(F32) for q in range(2)]

    def g1():
        val = g_line(2, 0)
        for q in range(2):
            p1s[q] = val[q].astype(BF16)
            send(p1s.at[q], p1r.at[q], g_s.at[4 + q], g_r.at[4 + q], at(1 - 2 * q, 0))

    def g_2(q):
        val = g_line(1 - 2 * q, 1 + q)
        arrived(p1r.at[q], g_s.at[4 + q], g_r.at[4 + q])
        p2s[q, :, q] = (val[q] + p1r[q].astype(F32)).astype(BF16)
        p2s[q, :, 1 - q] = val[1 - q].astype(BF16)
        send(p2s.at[q], p2r.at[q], g_s.at[6 + q], g_r.at[6 + q], at(1 - 2 * q, 0))

    def g3():
        val = g_line(0, 3)
        for q in range(2):
            arrived(p2r.at[q], g_s.at[6 + q], g_r.at[6 + q])
        for q in range(2):
            g2[:, q] = val[q] + p2r[0, :, q].astype(F32) + p2r[1, :, q].astype(F32)
        opp = wrap(r + 2, 4)
        for q in range(2):
            q1s[q] = g2[opp, q].astype(BF16)
            send(q1s.at[q], q1r.at[q], g_s.at[8 + q], g_r.at[8 + q], at(0, 1 - 2 * q))

    def g4():
        for q in range(2):
            rr = wrap(r + 1 - 2 * q, 4)
            arrived(q1r.at[q], g_s.at[8 + q], g_r.at[8 + q])
            q2s[q, q] = (g2[rr, q] + q1r[q].astype(F32)).astype(BF16)
            q2s[q, 1 - q] = g2[rr, 1 - q].astype(BF16)
            send(q2s.at[q], q2r.at[q], g_s.at[10 + q], g_r.at[10 + q], at(0, 1 - 2 * q))

    def g5():
        for q in range(2):
            arrived(q2r.at[q], g_s.at[10 + q], g_r.at[10 + q])
        fin[...] = (g2[r] + q2r[0].astype(F32) + q2r[1].astype(F32)).astype(BF16)
        send(fin.at[:, other, :], fing.at[c], g_s.at[12], g_r.at[12], sib)

    def g6():
        fing[c] = fin[:, mine, :]
        arrived(fing.at[1 - c], g_s.at[12], g_r.at[12])
        for h in range(2):
            for q in range(2):
                gt_ref[:, (h * 2 + q) * QW:(h * 2 + q + 1) * QW] = nn(place, fing[h, q]).astype(BF16)

    def r_send(k):
        send(rps.at[k], rpr.at[k], rt_s.at[k], rt_r.at[k], hyper[k])

    def r_got(k):
        arrived(rpr.at[k], rt_s.at[k], rt_r.at[k])
        rps[k + 1] = rps[k] + rpr[k]

    def r_out():
        total = rps[5, pl.ds(y * 4 + x, 1), :]
        column = jnp.broadcast_to(total, (n, n)).T
        lanes = (slot_r + (c * SL).astype(F32) == row_i.astype(F32)) & (routed_r > 0.5)
        gr_ref[...] = jnp.sum(jnp.where(lanes, column, 0.0), axis=0, keepdims=True)

    z_step(1)
    r_send(0)
    g_sib(0)
    g_sib(1)
    z_step(2)
    r_got(0)
    r_send(1)
    g_sib(2)
    g_sib(3)
    g1()
    r_got(1)
    r_send(2)
    z_unit(3, 2)
    g_2(0)
    z_unit(3, 0)
    g_2(1)
    z_unit(3, 1)
    r_got(2)
    r_send(3)
    g3()
    z_unit(4, 2)
    r_got(3)
    r_send(4)
    g4()
    z_unit(4, 0)
    z_unit(4, 1)
    r_got(4)
    r_out()
    g5()
    g6()
    for u in units:
        z_last(u)
    for u in units:
        z_out(u)
    for cp in sent:
        cp.wait_send()


def shards(
    tokens, cotangent, route_ids, route_weight, segment_ids, gate_weight, up_weight, down_weight
):
    vmem = pl.BlockSpec(memory_space=pltpu.VMEM)
    hbm = pl.BlockSpec(memory_space=pl.ANY)
    d = tokens.shape[2]
    dma = pltpu.SemaphoreType.DMA
    scratch = [
        pltpu.VMEM((2, 16, 2, 64, QW), BF16),
        pltpu.VMEM((2, 16, 2, 64, QW), BF16),
        pltpu.VMEM((32, SL + 16, 128), BF16),
        pltpu.VMEM((2, 8, 128), F32),
        pltpu.VMEM((d, 2 * FH), BF16),
        pltpu.VMEM((d, FH), BF16),
        pltpu.VMEM((1024, 2 * FH), F32),
        pltpu.VMEM((4, 2, 128, 2 * FH), BF16),
        pltpu.VMEM((3 * FH, 1024), BF16),
        pltpu.VMEM((2, NZ // 2, 3, FH, ZW), BF16),
        pltpu.VMEM((2, NZ // 2, 3, FH, ZW), BF16),
        pltpu.VMEM((4, 4, 2, 64, QW), BF16),
        pltpu.VMEM((4, 4, 2, 64, QW), BF16),
        pltpu.VMEM((2, 4, 64, QW), BF16),
        pltpu.VMEM((2, 4, 64, QW), BF16),
        pltpu.VMEM((2, 4, 2, 64, QW), BF16),
        pltpu.VMEM((2, 4, 2, 64, QW), BF16),
        pltpu.VMEM((4, 2, 64, QW), F32),
        pltpu.VMEM((2, 64, QW), BF16),
        pltpu.VMEM((2, 64, QW), BF16),
        pltpu.VMEM((2, 2, 64, QW), BF16),
        pltpu.VMEM((2, 2, 64, QW), BF16),
        pltpu.VMEM((2, 64, QW), BF16),
        pltpu.VMEM((2, 2, SL, QW), BF16),
        pltpu.VMEM((6, 16, 128), F32),
        pltpu.VMEM((5, 16, 128), F32),
        pltpu.VMEM((3, ZW, FH), F32),
        pltpu.VMEM((3, 192, FH), BF16),
        pltpu.VMEM((3, 192, FH), BF16),
        dma((3,)),
        dma((2, 20)), dma((2, 20)),
        dma((2, 18)), dma((2, 18)),
        dma((5,)), dma((5,)),
        dma((2, NZ // 2, 3)), dma((2, NZ // 2, 3)),
        dma((13,)), dma((13,)),
        dma((5,)), dma((5,)),
        dma((3,)), dma((3,)),
    ]
    shape = jax.ShapeDtypeStruct
    grads = shape((192, 2 * FH), F32)
    gt, gr, gg, gu, gd = pl.pallas_call(
        kernel,
        out_shape=(shape((128, d), BF16), shape((1, 128), F32), grads, grads, grads),
        in_specs=[vmem] * 5 + [hbm] * 3,
        out_specs=(vmem,) * 5,
        scratch_shapes=scratch,
        compiler_params=pltpu.CompilerParams(
            collective_id=0, has_side_effects=True, vmem_limit_bytes=62 * 1024 * 1024),
        cost_estimate=pl.CostEstimate(
            flops=13 * 10**9, bytes_accessed=14 * 10**6, transcendentals=1024 * FH),
    )(tokens[0], cotangent[0], route_ids[0], route_weight[0], segment_ids,
      gate_weight, up_weight, down_weight)
    return gt[None], gr, gg, gu, gd


def solution(mesh):
    return jax.shard_map(
        shards,
        mesh=mesh,
        in_specs=(
            P("dp", "et", None),
            P("dp", "et", None),
            P("dp", "et", None),
            P("dp", "et", None),
            P("dp", "et"),
            P(None, "et"),
            P(None, "et"),
            P(None, "et"),
        ),
        out_specs=(P("dp", "et", None), P("dp", "et"), P("dp", "et"), P("dp", "et"), P("dp", "et")),
        check_vma=False,
    )
```

time: 543 us -> 134 us (0.25)
  waiting for transfers between devices: 381 us -> 0 us
  Pallas kernels: 0 us -> 123 us
  blocking collectives: 85.8 us -> 0 us
  matrix products: 28 us -> 0 us
  other arithmetic: 23.1 us -> 0 us
  between operations: 15.3 us -> 0.65 us
    reduce_scatter x2 -> x0, waiting for transfers between devices: 340 us -> none  [the longest x1 315 us: shards(): lax.psum_scatter(jnp.concatenate([rounded_partial(contract_rows(rows_in,...]
    pallas_call x0 -> x1, Pallas kernels: none -> 123 us  [shards(): pl.pallas_call(kernel, out_shape=(shape((128, d), BF16), shape((1, 128),...]
    unnamed x2 -> x0, blocking collectives: 56 us -> none
    all_gather x2 -> x0, waiting for transfers between devices: 40.3 us -> none  [the longest x1 33.3 us: shards(): lax.all_gather(packed_cot, 'et', axis=0, tiled=True)]
    psum x1 -> x0, blocking collectives: 29.7 us -> none  [shards(): counts = lax.psum(jnp.sum(member, axis=0), 'et')]
    dot_general x8 -> x0, matrix products: 28 us -> none  [the longest x3 8.38 us: contract_rows(): lax.dot_general(left, right, (((0,), (0,)), ((), ())), preferred_element_...]
    unnamed x29 -> x9, local copies, waits for them, and re-layouts: 1.3 us -> 10.3 us
    concatenate x1 -> x0, other arithmetic: 7.23 us -> none  [shards(): jnp.concatenate([rounded_partial(contract_rows(rows_in, grad_gate_rows)),...]
  transfers between devices with their start and end apart: 4 -> 0, of which waited for: 4 -> 0; matrix products, arithmetic and copies ran while one was open for 6% -> 0% of each run, Pallas kernels for 0% -> 0%
where the time goes in v1:
time: 134 us
  Pallas kernels  123 us (92%)
  local copies, waits for them, and re-layouts  10.3 us (8%)
    pallas_call x1, Pallas kernels, shards(): pl.pallas_call(kernel, out_shape=(shape((128, d), BF16), shape((1, 128),...  123 us
    unnamed x9, local copies, waits for them, and re-layouts  10.3 us

profile of v1, /device:TPU:1, one launch (start us, length us, event | category | flops | bytes accessed | tf_op | source)
XLA Modules:
  0.0 133.7 jit_solution(1575594436198438324)
XLA Ops:
  0.6 1.4 %copy.14 = bf16[1,128,2]{2,1,0:T(8,128)(2,1)} copy(bf16[1,128,2]{1,2,0:T(2,128)(2,1)} %param.11) | data formatting | bytes 1024 | tf_op args[3]
  2.0 1.4 %copy.13 = s32[1,128,2]{2,1,0:T(8,128)} copy(s32[1,128,2]{1,2,0:T(2,128)} %param.10) | data formatting | bytes 2048 | tf_op args[2]
  3.4 122.7 %shard_map.119 = (bf16[128,3072]{1,0:T(8,128)(2,1)}, f32[1,128]{1,0:T(1,128)}, f32[192,512]{1,0:T(8,128)}, f32[192,512]{1,0:T(8,128)}, f32[192,512]{1,0:T(8,128)}) custom-call(bf16[128,3072]{1,0:T(8,128)(2,1)} %bitcast.8, bf16[128,3072]{1,0:T(8,128)(2,1)} %bitcast.9, s32[128,2]{1,0:T(8,128)} %bitcast.6, bf16[128,2]{1,0:T(8,128)(2,1)} %bitcast.7, ...), custom_call_target="tpu_custom_call" | custom-call | flops 12999999488 | bytes 14000000 | tf_op jit(solution)/shard_map/pallas_call | solution.py:534
  126.1 0.0 copy-start
  126.2 2.1 %copy.20 = bf16[1,128,3072]{2,1,0:T(8,128)(2,1)} copy(bf16[1,128,3072]{2,1,0:T(8,128)(2,1)} %bitcast.5) | data formatting | bytes 1572864
  128.3 1.1 copy.21
  129.4 1.8 %copy.22 = f32[192,512]{1,0:T(8,128)} copy(f32[192,512]{1,0:T(8,128)} %get-tuple-element.22) | data formatting | bytes 786432
  131.2 1.8 %copy.23 = f32[192,512]{1,0:T(8,128)} copy(f32[192,512]{1,0:T(8,128)} %get-tuple-element.23) | data formatting | bytes 786432
  132.9 0.0 copy-done
  132.9 0.7 copy.24
Async XLA Ops:
  126.1 6.8 %copy-start = (f32[192,512]{1,0:T(8,128)S(1)}, f32[192,512]{1,0:T(8,128)}, u32[]{:S(2)}) copy-start(f32[192,512]{1,0:T(8,128)} %get-tuple-element.24) | copy-start | bytes 1179652

commit v2 on v1

--- a/solution.py
+++ b/solution.py
@@ -30,9 +30,9 @@
 def kernel(
     tok_ref, cot_ref, ids_ref, rw_ref, seg_ref, wg_hbm, wu_hbm, wd_hbm,
     gt_ref, gr_ref, gg_ref, gu_ref, gd_ref,
-    tb, cb, meta, cnt, wgu, wd, pre, dgu, dT, zs, zr, sgs, sgr, p1s, p1r, p2s, p2r, g2,
+    tb, cb, cnts, wgu, wd, pre, hidb, backb, dgu, dT, zs, zr, sgs, sgr, p1s, p1r, p2s, p2r, g2,
     q1s, q1r, q2s, q2r, fin, fing, rps, rpr, fsum, fxs, fxr,
-    w_sem, ag_s, ag_r, sib_s, sib_r, m_s, m_r, z_s, z_r, g_s, g_r, rt_s, rt_r, fx_s, fx_r,
+    w_sem, ag_s, ag_r, sib_s, sib_r, sw_s, sw_r, m_s, m_r, z_s, z_r, g_s, g_r, rt_s, rt_r, fx_s, fx_r,
 ):
     dp, et = lax.axis_index("dp"), lax.axis_index("et")
     z, yh = lax.div(dp, 2), lax.rem(dp, 2)
@@ -70,7 +70,10 @@
         cp.start()
 
     barrier = pltpu.get_barrier_semaphore()
-    for nb in (sib, at(1, 0), at(-1, 0), at(0, 1), at(0, -1), at(2, 0), at(0, 2), zplus, zminus):
+    group = [dev(wrap(x + a, 4), yh * 2 + wrap(yl + b, 2), z, wrap(c + e, 2))
+             for a in range(4) for b in range(2) for e in range(2)][1:]
+    outer = dev(x, wrap(y + 2 * yl - 1, 4), z, c)
+    for nb in (*group, outer, partner, zplus, zminus):
         pl.semaphore_signal(barrier, inc=1, device_id=nb, device_id_type=MESH)
 
     sent = []
@@ -91,77 +94,84 @@
     row_i = lax.broadcasted_iota(jnp.int32, (n, n), 0)
     col_i = lax.broadcasted_iota(jnp.int32, (n, n), 1)
     chosen = ids_ref[...] == 0
-    routed = jnp.max(chosen.astype(F32), axis=1, keepdims=True)
-    prob = jnp.sum(jnp.where(chosen, rw_ref[...].astype(F32), 0.0), axis=1, keepdims=True)
-    routed_c = jnp.broadcast_to(routed, (n, n))
-    routed_r = routed_c.T
+    routed = jnp.max(chosen.astype(F32), axis=0, keepdims=True)
+    prob = jnp.sum(jnp.where(chosen, rw_ref[...].astype(F32), 0.0), axis=0, keepdims=True)
+    routed_r = jnp.broadcast_to(routed, (n, n))
+    routed_c = routed_r.T
     before = (row_i < col_i).astype(F32).astype(BF16)
     after = (col_i < row_i).astype(F32).astype(BF16)
     slot_r = nn(routed_r.astype(BF16), before)
     slot_c = nn(after, routed_c.astype(BF16))
     pick = jnp.where((slot_r == row_i.astype(F32)) & (routed_r > 0.5), 1.0, 0.0)[:SL].astype(BF16)
     place = jnp.where((slot_c == col_i.astype(F32)) & (routed_c > 0.5), 1.0, 0.0)[:, :SL].astype(BF16)
+    seg = jnp.broadcast_to(seg_ref[...], (n, n))
+    member = jnp.where(seg == row_i, 1.0, 0.0).astype(BF16)
+    cnts[et] = nt(jnp.ones((8, n), BF16), member)
 
     mine = pl.ds(pl.multiple_of(c * SL, SL), SL)
+    other = pl.ds(pl.multiple_of((1 - c) * SL, SL), SL)
     here = p * 4 + r
     there = r * 4 + p
 
-    def pack(src, buf):
+    for h in range(2):
+        for q in range(2):
+            cols = slice((h * 2 + q) * QW, (h * 2 + q + 1) * QW)
+            tb[h, here, q, mine, :] = nn(pick, tok_ref[:, cols]).astype(BF16)
+
+    pl.semaphore_wait(barrier, len(group) + 4)
+    for k, nb in enumerate(group):
+        send(cnts.at[et], cnts.at[et], m_s.at[k], m_r.at[k], nb)
+
+    def tok_rows(h, rows):
+        return tb.at[h, here, :, rows, :], tb.at[h, there, :, rows, :]
+
+    def cot_rows(h, rows):
+        return cb.at[h, :, here, :, rows, :], cb.at[h, :, there, :, rows, :]
+
+    def swap(t, rows_of):
+        for k, h in ((0, 1 - c), (1, c)):
+            src, dst = rows_of(h, mine)
+            send(src, dst, sw_s.at[t, k], sw_r.at[t, k], sib)
+
+    def swapped(t, rows_of, k):
+        h = c if k == 0 else 1 - c
+        arrived(rows_of(h, other)[0], sw_s.at[t, k], sw_r.at[t, k])
+
+    swap(0, tok_rows)
+
+    def far_first(h, k, j):
+        return wrap(z + (4 - 2 * k - j if h == 0 else 2 * k + j - 3), NZ)
+
+    def pack_cot():
+        for k, nb in enumerate(group):
+            arrived(cnts.at[0], m_s.at[k], m_r.at[k])
+        total = jnp.sum(cnts[...], axis=0)[0:1]
+        slot_count = jnp.sum(nt(pick, member) * total, axis=1, keepdims=True)
+        slot_prob = jnp.sum(nt(pick, jnp.where(row_i == 16, prob, 0.0).astype(BF16)), axis=1, keepdims=True)
+        scale = jnp.where(slot_count > 0.0, slot_prob / jnp.maximum(slot_count, 1.0), 0.0)
         for h in range(2):
-            for q in range(2):
-                cols = slice((h * 2 + q) * QW, (h * 2 + q + 1) * QW)
-                buf[h, here, q, mine, :] = nn(pick, src[:, cols]).astype(BF16)
-
-    def swap(t, buf):
-        for k, h in ((0, 1 - c), (1, c)):
-            send(buf.at[h, here, :, mine, :], buf.at[h, there, :, mine, :],
-                 sib_s.at[t, 16 + k], sib_r.at[t, 16 + k], sib)
-
-    other = pl.ds(pl.multiple_of((1 - c) * SL, SL), SL)
-
-    def swapped(t, buf, k):
-        h = c if k == 0 else 1 - c
-        arrived(buf.at[h, here, :, other, :], sib_s.at[t, 16 + k], sib_r.at[t, 16 + k])
-
-    me_idx = (y * 4 + x) * 2 + c
-    seg = jnp.broadcast_to(seg_ref[...], (n, n))
-    member = jnp.where(seg == row_i, 1.0, 0.0).astype(BF16)
-    prob_m = jnp.where(col_i == 16, jnp.broadcast_to(prob, (n, n)), 0.0).astype(BF16)
-    meta[me_idx, pl.ds(0, SL), :] = (nt(pick, member) + nn(pick, prob_m)).astype(BF16)
-    meta[me_idx, pl.ds(SL, 16), :] = nt(jnp.ones((16, n), BF16), member).astype(BF16)
-
-    pack(tok_ref, tb)
-    pl.semaphore_wait(barrier, 9)
-    swap(0, tb)
-
-    def meta_send(k):
-        size = 1 << k
-        base = lax.div(me_idx, size) * size
-        ref = meta.at[pl.ds(base, size)]
-        send(ref, ref, m_s.at[k], m_r.at[k], hyper[k])
-
-    def meta_got(k):
-        size = 1 << k
-        base = flip(lax.div(me_idx, size), 1) * size
-        arrived(meta.at[pl.ds(base, size)], m_s.at[k], m_r.at[k])
-
-    meta_send(0)
-    pack(cot_ref, cb)
+            for k in range(2):
+                for j in range(2):
+                    cols = pl.ds(pl.multiple_of(far_first(h, k, j) * ZW, 128), ZW)
+                    cb[h, k, here, j, mine, :] = (nn(pick, cot_ref[:, cols]) * scale).astype(BF16)
+        swap(1, cot_rows)
 
     line = (0, -1, 1, 2)
 
-    def ag(t, buf):
+    def ag(t, at_core):
+        def ref_of(h, place_, q):
+            return at_core(h, place_) if q is None else at_core(h, place_).at[q]
+
         def one(dst_p, dst_r, q, k, to):
-            ref = buf.at[c, pos(dst_p, dst_r)] if q is None else buf.at[c, pos(dst_p, dst_r), q]
+            ref = ref_of(c, pos(dst_p, dst_r), q)
             send(ref, ref, ag_s.at[t, k], ag_r.at[t, k], to)
 
         def got(dst_p, dst_r, q, k):
-            ref = buf.at[c, pos(dst_p, dst_r)] if q is None else buf.at[c, pos(dst_p, dst_r), q]
-            arrived(ref, ag_s.at[t, k], ag_r.at[t, k])
+            arrived(ref_of(c, pos(dst_p, dst_r), q), ag_s.at[t, k], ag_r.at[t, k])
 
         def to_sib(a, b):
-            k = (a % 4) * 4 + b % 4
-            send(buf.at[c, pos(a, b)], buf.at[c, wrap(r + b, 4) * 4 + wrap(p + a, 4)],
+            k = (a % 4) * 4 + b % 4 - 1
+            send(at_core(c, pos(a, b)), at_core(c, wrap(r + b, 4) * 4 + wrap(p + a, 4)),
                  sib_s.at[t, k], sib_r.at[t, k], sib)
 
         def out_p(j):
@@ -206,46 +216,15 @@
             for a in range(4):
                 for b in range(4):
                     if a or b:
-                        k = a * 4 + b
-                        arrived(buf.at[1 - c, pos(b, a)], sib_s.at[t, k], sib_r.at[t, k])
-            swapped(t, buf, 1)
+                        k = a * 4 + b - 1
+                        arrived(at_core(1 - c, pos(b, a)), sib_s.at[t, k], sib_r.at[t, k])
 
         return begin, first, second, near, far, from_sib
 
-    T, C = ag(0, tb), ag(1, cb)
-    swapped(0, tb, 0)
-    T[0]()
-    swap(1, cb)
-    meta_got(0)
-    meta_send(1)
-    T[1]()
-    meta_got(1)
-    meta_send(2)
-    T[2]()
-    swapped(1, cb, 0)
-    meta_got(2)
-    meta_send(3)
-    T[3](0)
-    C[0]()
-    T[3](1)
-    meta_got(3)
-    meta_send(4)
-    T[4](0)
-    T[3](2)
-    T[4](1)
-    T[3](3)
-    T[4](2)
-    T[4](3)
-    C[1]()
-    T[5]()
-    C[2]()
-    meta_got(4)
-
-    for g in range(2):
-        cnt[g] = jnp.sum(meta[pl.ds(16 * g, 16), pl.ds(SL, 16), :].astype(F32), axis=0)[:8]
-
-    for cp in wcopies:
-        cp.wait()
+    T = ag(0, lambda h, i: tb.at[h, i])
+    C1 = ag(1, lambda h, i: cb.at[h, 0, i])
+    C2 = ag(2, lambda h, i: cb.at[h, 1, i])
+    BEGIN, FIRST, SECOND, NEAR, FAR, FROM_SIB = range(6)
 
     def fwd(i):
         rows = pl.ds(pl.multiple_of(i * 256, 256), 256)
@@ -253,71 +232,62 @@
         for h in range(2):
             for q in range(2):
                 xs = tb[h, pl.ds(i * 4, 4), q].reshape(256, QW)
-                part = nn(xs, wgu[(h * 2 + q) * QW:(h * 2 + q + 1) * QW, :])
-                acc = part if acc is None else acc + part
+                one = nn(xs, wgu[(h * 2 + q) * QW:(h * 2 + q + 1) * QW, :])
+                acc = one if acc is None else acc + one
         pre[rows, :] = acc
 
-    C[3](0)
-    fwd(0)
-    C[3](1)
-    C[4](0)
-    fwd(1)
-    C[3](2)
-    C[4](1)
-    fwd(2)
-    C[3](3)
-    C[4](2)
-    fwd(3)
-    C[4](3)
-    C[5]()
-
-    lane = lax.broadcasted_iota(jnp.int32, (n, n), 1)
-
-    @pl.loop(0, 8)
-    def _(j):
-        rows = pl.ds(pl.multiple_of(j * n, n), n)
-        back = None
+    def activate(i):
+        for j in (2 * i, 2 * i + 1):
+            rows = pl.ds(j * n, n)
+            gate, up = pre[rows, 0:FH], pre[rows, FH:2 * FH]
+            sg = 1.0 / (1.0 + jnp.exp(-gate))
+            act = gate * sg
+            hid = act * up
+            pre[rows, 0:FH] = up * (sg * (1.0 + gate * (1.0 - sg)))
+            pre[rows, FH:2 * FH] = act
+            hidb[rows, :] = hid
+            dT[2 * FH:3 * FH, rows] = hid.T.astype(BF16)
+
+    def back_part(k, i):
+        rows = pl.ds(i * 256, 256)
+        acc = None
         for h in range(2):
-            for q in range(2):
-                xs = cb[h, pl.ds(j * 2, 2), q].reshape(n, QW)
-                part = nn(xs, wd[(h * 2 + q) * QW:(h * 2 + q + 1) * QW, :])
-                back = part if back is None else back + part
-        chips, metas, counts = [], [], []
+            for j in range(2):
+                xs = cb[h, k, pl.ds(i * 4, 4), j].reshape(256, ZW)
+                one = nn(xs, wd[pl.ds(pl.multiple_of(far_first(h, k, j) * ZW, ZW), ZW), :])
+                acc = one if acc is None else acc + one
+        if k == 0:
+            backb[rows, :] = acc
+        else:
+            backb[rows, :] += acc
+
+    lane1 = lax.broadcasted_iota(jnp.int32, (1, n), 1)
+
+    def gradients(j):
+        rows = pl.ds(j * n, n)
+        back = backb[rows, :]
+        dg, du = back * pre[rows, 0:FH], back * pre[rows, FH:2 * FH]
+        dgu[j // 2, j % 2, :, 0:FH] = dg.astype(BF16)
+        dgu[j // 2, j % 2, :, FH:2 * FH] = du.astype(BF16)
+        dT[0:FH, rows] = dg.T.astype(BF16)
+        dT[FH:2 * FH, rows] = du.T.astype(BF16)
+        rp = jnp.sum(hidb[rows, :] * back, axis=1, keepdims=True)
+        rp_row = jnp.broadcast_to(rp, (n, n)).T[0:1]
         for k in range(2):
             i = j * 2 + k
-            chip = i + c * (lax.rem(i, 4) * 4 + lax.div(i, 4) - i)
-            m = meta[pl.ds(chip * 2, 2), pl.ds(0, SL), :].astype(F32).reshape(2 * SL, n)
-            chips.append(chip)
-            metas.append(m)
-            counts.append(jnp.where(lane[:64] < 8, m * cnt[lax.div(chip, 8)][0:1], 0.0))
-        m = jnp.concatenate(metas, axis=0)
-        count = jnp.sum(jnp.concatenate(counts, axis=0), axis=1, keepdims=True)
-        weight = jnp.where(count > 0.0, 1.0 / jnp.maximum(count, 1.0), 0.0)
-        pr = jnp.sum(jnp.where(lane == 16, m, 0.0), axis=1, keepdims=True)
-        gate, up = pre[rows, 0:FH], pre[rows, FH:2 * FH]
-        back = back * weight
-        sg = 1.0 / (1.0 + jnp.exp(-gate))
-        act = gate * sg
-        slope = sg * (1.0 + gate * (1.0 - sg))
-        hid = act * up
-        rp = jnp.sum(hid * back, axis=1, keepdims=True)
-        sb = back * pr
-        dg = sb * up * slope
-        du = sb * act
-        he = hid * (pr * weight)
-        dgu[lax.div(j, 2), lax.rem(j, 2), :, 0:FH] = dg.astype(BF16)
-        dgu[lax.div(j, 2), lax.rem(j, 2), :, FH:2 * FH] = du.astype(BF16)
-        dT[0:FH, rows] = dg.T.astype(BF16)
-        dT[FH:2 * FH, rows] = du.T.astype(BF16)
-        dT[2 * FH:3 * FH, rows] = he.T.astype(BF16)
-        rp_row = jnp.broadcast_to(rp, (n, n)).T[0:1]
-        rps[0, pl.ds(chips[0], 1), :] = jnp.where(lane[0:1] < 64, rp_row, 0.0)
-        rps[0, pl.ds(chips[1], 1), :] = jnp.where(lane[0:1] < 64, pltpu.roll(rp_row, 64, 1), 0.0)
+            chip = i + c * (i % 4 * 4 + i // 4 - i)
+            row = rp_row if k == 0 else pltpu.roll(rp_row, 64, 1)
+            rps[0, pl.ds(chip, 1), :] = jnp.where(lane1 < 64, row, 0.0)
 
     def part(u, d):
-        buf = cb if u == 2 else tb
-        cols = pl.ds(pl.multiple_of(lax.rem(d, 2) * ZW, 128), ZW)
-        xs = buf[lax.div(d, 4), :, lax.rem(lax.div(d, 2), 2), :, cols].reshape(1024, ZW)
+        if u == 2:
+            h = 0 if 1 <= d <= 4 else 1
+            i = 4 - d if h == 0 else d + 3
+            xs = cb[h, i // 2, :, i % 2].reshape(1024, ZW)
+        else:
+            d = wrap(z + d, NZ)
+            cols = pl.ds(pl.multiple_of(lax.rem(d, 2) * ZW, 128), ZW)
+            xs = tb[lax.div(d, 4), :, lax.rem(lax.div(d, 2), 2), :, cols].reshape(1024, ZW)
         return nn(dT[u * FH:(u + 1) * FH, :], xs)
 
     units = (2, 0, 1)
@@ -326,14 +296,14 @@
 
     def z_unit(s, u):
         if s == 1:
-            val = part(u, wrap(z + STEPS, NZ)).astype(BF16)
+            val = part(u, STEPS).astype(BF16)
             for dr, to in ((0, zplus), (1, zminus)):
                 zs[dr, 0, u, dr * HF:(dr + 1) * HF, :] = val[dr * HF:(dr + 1) * HF]
                 ref = (dr, 0, u, pl.ds(dr * HF, HF))
                 send(zs.at[ref], zr.at[ref], z_s.at[dr, 0, u], z_r.at[dr, 0, u], to)
             return
         for dr, to, off in ((0, zplus, STEPS + 1 - s), (1, zminus, s - STEPS - 1)):
-            val = part(u, wrap(z + off, NZ))
+            val = part(u, off)
             if s == 2:
                 ref = zr.at[dr, 0, u, pl.ds(dr * HF, HF)]
                 arrived(ref, z_s.at[dr, 0, u], z_r.at[dr, 0, u])
@@ -356,7 +326,7 @@
     yourcols = pl.ds(pl.multiple_of((1 - yh) * FH, FH), FH)
 
     def z_last(u):
-        val = part(u, z)
+        val = part(u, 0)
         for dr in range(2):
             ref = zr.at[dr, STEPS - 1, u]
             arrived(ref, z_s.at[dr, STEPS - 1, u], z_r.at[dr, STEPS - 1, u])
@@ -443,44 +413,130 @@
         total = rps[5, pl.ds(y * 4 + x, 1), :]
         column = jnp.broadcast_to(total, (n, n)).T
         lanes = (slot_r + (c * SL).astype(F32) == row_i.astype(F32)) & (routed_r > 0.5)
-        gr_ref[...] = jnp.sum(jnp.where(lanes, column, 0.0), axis=0, keepdims=True)
-
-    z_step(1)
+        summed = jnp.sum(jnp.where(lanes, column, 0.0), axis=0, keepdims=True)
+        gr_ref[...] = jnp.where(routed > 0.5, summed / jnp.maximum(prob, 0.25), 0.0)
+
+    GATE, UP, DOWN = 0, 1, 2
+    swapped(0, tok_rows, 0)
+    T[BEGIN]()
+    pack_cot()
+    swapped(1, cot_rows, 0)
+    C1[BEGIN]()
+    T[FIRST]()
+    T[NEAR](0)
+    T[SECOND]()
+    C1[FIRST]()
+    C1[NEAR](0)
+    T[NEAR](1)
+    T[NEAR](2)
+    T[FAR](0)
+    C1[SECOND]()
+    T[NEAR](3)
+    T[FAR](1)
+    T[FAR](2)
+    C2[BEGIN]()
+    C1[NEAR](1)
+    T[FAR](3)
+    swapped(0, tok_rows, 1)
+    T[FROM_SIB]()
+    for cp in wcopies:
+        cp.wait()
+    fwd(0)
+    C1[NEAR](2)
+    C1[FAR](0)
+    fwd(1)
+    C2[FIRST]()
+    C2[NEAR](0)
+    fwd(2)
+    C1[NEAR](3)
+    C1[FAR](1)
+    C1[FAR](2)
+    fwd(3)
+    C2[SECOND]()
+    activate(0)
+    activate(1)
+    C1[FAR](3)
+    C2[NEAR](1)
+    C2[NEAR](2)
+    activate(2)
+    activate(3)
+    C2[FAR](0)
+    swapped(1, cot_rows, 1)
+    C1[FROM_SIB]()
+    z_unit(1, DOWN)
+    C2[NEAR](3)
+    for i in range(4):
+        back_part(0, i)
+    C2[FAR](1)
+    C2[FAR](2)
+    z_unit(2, DOWN)
+    C2[FAR](3)
+    C2[FROM_SIB]()
+    z_unit(3, DOWN)
+    for i in range(4):
+        back_part(1, i)
+        gradients(2 * i)
+        gradients(2 * i + 1)
+    z_unit(1, GATE)
+    z_unit(1, UP)
     r_send(0)
     g_sib(0)
+    g1()
+    z_unit(4, DOWN)
     g_sib(1)
-    z_step(2)
     r_got(0)
     r_send(1)
+    z_unit(2, GATE)
     g_sib(2)
-    g_sib(3)
-    g1()
+    z_unit(2, UP)
     r_got(1)
     r_send(2)
-    z_unit(3, 2)
     g_2(0)
-    z_unit(3, 0)
     g_2(1)
-    z_unit(3, 1)
+    g_sib(3)
+    z_unit(3, GATE)
     r_got(2)
     r_send(3)
     g3()
-    z_unit(4, 2)
+    z_unit(3, UP)
+    z_last(DOWN)
     r_got(3)
     r_send(4)
     g4()
-    z_unit(4, 0)
-    z_unit(4, 1)
+    z_unit(4, GATE)
     r_got(4)
     r_out()
     g5()
+    z_unit(4, UP)
+    z_out(DOWN)
     g6()
-    for u in units:
-        z_last(u)
-    for u in units:
-        z_out(u)
+    z_last(GATE)
+    z_last(UP)
+    z_out(GATE)
+    z_out(UP)
     for cp in sent:
         cp.wait_send()
+
+
+def copies(*refs):
+    ins, outs, sem = refs[:5], refs[5:10], refs[10]
+    moves = [pltpu.make_async_copy(a, b, sem.at[k]) for k, (a, b) in enumerate(zip(ins, outs))]
+    for cp in moves:
+        cp.start()
+    for cp in moves:
+        cp.wait()
+
+
+def hand_over(*arrays):
+    hbm = pl.BlockSpec(memory_space=pl.ANY)
+    return pl.pallas_call(
+        copies,
+        out_shape=tuple(jax.ShapeDtypeStruct(a.shape, a.dtype) for a in arrays),
+        in_specs=[hbm] * 5,
+        out_specs=(hbm,) * 5,
+        scratch_shapes=[pltpu.SemaphoreType.DMA((5,))],
+        compiler_params=pltpu.CompilerParams(vmem_limit_bytes=62 * 1024 * 1024),
+    )(*arrays)
 
 
 def shards(
@@ -492,12 +548,13 @@
     dma = pltpu.SemaphoreType.DMA
     scratch = [
         pltpu.VMEM((2, 16, 2, 64, QW), BF16),
-        pltpu.VMEM((2, 16, 2, 64, QW), BF16),
-        pltpu.VMEM((32, SL + 16, 128), BF16),
-        pltpu.VMEM((2, 8, 128), F32),
+        pltpu.VMEM((2, 2, 16, 2, 64, ZW), BF16),
+        pltpu.VMEM((16, 8, 128), F32),
         pltpu.VMEM((d, 2 * FH), BF16),
         pltpu.VMEM((d, FH), BF16),
         pltpu.VMEM((1024, 2 * FH), F32),
+        pltpu.VMEM((1024, FH), F32),
+        pltpu.VMEM((1024, FH), F32),
         pltpu.VMEM((4, 2, 128, 2 * FH), BF16),
         pltpu.VMEM((3 * FH, 1024), BF16),
         pltpu.VMEM((2, NZ // 2, 3, FH, ZW), BF16),
@@ -521,9 +578,10 @@
         pltpu.VMEM((3, 192, FH), BF16),
         pltpu.VMEM((3, 192, FH), BF16),
         dma((3,)),
-        dma((2, 20)), dma((2, 20)),
-        dma((2, 18)), dma((2, 18)),
-        dma((5,)), dma((5,)),
+        dma((3, 20)), dma((3, 20)),
+        dma((3, 15)), dma((3, 15)),
+        dma((2, 2)), dma((2, 2)),
+        dma((15,)), dma((15,)),
         dma((2, NZ // 2, 3)), dma((2, NZ // 2, 3)),
         dma((13,)), dma((13,)),
         dma((5,)), dma((5,)),
@@ -541,8 +599,9 @@
             collective_id=0, has_side_effects=True, vmem_limit_bytes=62 * 1024 * 1024),
         cost_estimate=pl.CostEstimate(
             flops=13 * 10**9, bytes_accessed=14 * 10**6, transcendentals=1024 * FH),
-    )(tokens[0], cotangent[0], route_ids[0], route_weight[0], segment_ids,
+    )(tokens[0], cotangent[0], route_ids[0].T, route_weight[0].T, segment_ids,
       gate_weight, up_weight, down_weight)
+    gt, gr, gg, gu, gd = hand_over(gt, gr, gg, gu, gd)
     return gt[None], gr, gg, gu, gd
 
 

time: 134 us -> 172 us (1.28)
  Pallas kernels: 123 us -> 171 us
  local copies, waits for them, and re-layouts: 10.3 us -> 0 us
    pallas_call x0 -> x1, Pallas kernels: none -> 60.7 us  [hand_over(): pl.pallas_call(copies, out_shape=tuple((jax.ShapeDtypeStruct(a.shape, a.d...]
    pallas_call x1, Pallas kernels: 123 us -> 110 us  [shards(): pl.pallas_call(kernel, out_shape=(shape((128, d), BF16), shape((1, 128),...]
    unnamed x9 -> x0, local copies, waits for them, and re-layouts: 10.3 us -> none
where the time goes in v2:
time: 172 us; the launch traced here: 171 us
  Pallas kernels  171 us (99%)
    pallas_call x1, Pallas kernels, shards(): pl.pallas_call(kernel, out_shape=(shape((128, d), BF16), shape((1, 128),...  110 us
    pallas_call x1, Pallas kernels, hand_over(): pl.pallas_call(copies, out_shape=tuple((jax.ShapeDtypeStruct(a.shape, a.d...  60.7 us

profile of v2, /device:TPU:1, one launch (start us, length us, event | category | flops | bytes accessed | tf_op | source)
XLA Modules:
  0.0 171.5 jit_solution(4960935417675258247)
XLA Ops:
  0.6 109.9 %shard_map.119 = (bf16[128,3072]{1,0:T(8,128)(2,1)}, f32[1,128]{1,0:T(1,128)}, f32[192,512]{1,0:T(8,128)}, f32[192,512]{1,0:T(8,128)}, f32[192,512]{1,0:T(8,128)}) custom-call(bf16[128,3072]{1,0:T(8,128)(2,1)} %bitcast.9, bf16[128,3072]{1,0:T(8,128)(2,1)} %bitcast.10, s32[2,128]{1,0:T(2,128)} %bitcast.12, bf16[2,128]{1,0:T(2,128)(2,1)} %bitcast.13, ...), custom_call_target="tpu_custom_call" | custom-call | flops 12999999488 | bytes 14000000 | tf_op jit(solution)/shard_map/pallas_call | solution.py:592
  110.6 60.7 %shard_map.120 = (bf16[128,3072]{1,0:T(8,128)(2,1)}, f32[1,128]{1,0:T(1,128)}, f32[192,512]{1,0:T(8,128)}, f32[192,512]{1,0:T(8,128)}, f32[192,512]{1,0:T(8,128)}) custom-call(bf16[128,3072]{1,0:T(8,128)(2,1)} %get-tuple-element.15.refs_0_, f32[1,128]{1,0:T(1,128)} %get-tuple-element.16.refs_1_, f32[192,512]{1,0:T(8,128)} %get-tuple-element.17.refs_2_, ...), custom_call_target="tpu_custom_call" | custom-call | tf_op jit(solution)/shard_map/pallas_call | solution.py:532

commit v3 on v2

--- a/solution.py
+++ b/solution.py
@@ -28,11 +28,12 @@
 
 
 def kernel(
-    tok_ref, cot_ref, ids_ref, rw_ref, seg_ref, wg_hbm, wu_hbm, wd_hbm,
-    gt_ref, gr_ref, gg_ref, gu_ref, gd_ref,
+    ids_ref, rw_ref, seg_ref, tok_hbm, cot_hbm, wg_hbm, wu_hbm, wd_hbm,
+    gt_hbm, gr_hbm, gg_hbm, gu_hbm, gd_hbm,
+    tok_ref, cot_ref, gt_ref, gr_ref, wob,
     tb, cb, cnts, wgu, wd, pre, hidb, backb, dgu, dT, zs, zr, sgs, sgr, p1s, p1r, p2s, p2r, g2,
     q1s, q1r, q2s, q2r, fin, fing, rps, rpr, fsum, fxs, fxr,
-    w_sem, ag_s, ag_r, sib_s, sib_r, sw_s, sw_r, m_s, m_r, z_s, z_r, g_s, g_r, rt_s, rt_r, fx_s, fx_r,
+    i_sem, o_sem, w_sem, ag_s, ag_r, sib_s, sib_r, sw_s, sw_r, m_s, m_r, z_s, z_r, g_s, g_r, rt_s, rt_r, fx_s, fx_r,
 ):
     dp, et = lax.axis_index("dp"), lax.axis_index("et")
     z, yh = lax.div(dp, 2), lax.rem(dp, 2)
@@ -60,23 +61,33 @@
              dev(x, flip(y, 1), z, c), dev(x, flip(y, 2), z, c)]
     partner = hyper[4]
 
+    icopies = [pltpu.make_async_copy(tok_hbm, tok_ref, i_sem.at[0]),
+               pltpu.make_async_copy(cot_hbm, cot_ref, i_sem.at[1])]
+    for cp in icopies:
+        cp.start()
+
     half = pl.ds(pl.multiple_of(yh * FH, FH), FH)
     wcopies = [
         pltpu.make_async_copy(wg_hbm.at[:, half], wgu.at[:, pl.ds(0, FH)], w_sem.at[0]),
         pltpu.make_async_copy(wu_hbm.at[:, half], wgu.at[:, pl.ds(FH, FH)], w_sem.at[1]),
         pltpu.make_async_copy(wd_hbm.at[:, half], wd, w_sem.at[2]),
     ]
-    for cp in wcopies:
-        cp.start()
-
     barrier = pltpu.get_barrier_semaphore()
     group = [dev(wrap(x + a, 4), yh * 2 + wrap(yl + b, 2), z, wrap(c + e, 2))
              for a in range(4) for b in range(2) for e in range(2)][1:]
     outer = dev(x, wrap(y + 2 * yl - 1, 4), z, c)
     for nb in (*group, outer, partner, zplus, zminus):
         pl.semaphore_signal(barrier, inc=1, device_id=nb, device_id_type=MESH)
+    for cp in wcopies:
+        cp.start()
 
     sent = []
+    written = []
+
+    def write(src, dst, k):
+        cp = pltpu.make_async_copy(src, dst, o_sem.at[k])
+        cp.start()
+        written.append(cp)
 
     def copy(src, dst, ss, rs, to):
         return pltpu.make_async_remote_copy(
@@ -113,6 +124,7 @@
     here = p * 4 + r
     there = r * 4 + p
 
+    icopies[0].wait()
     for h in range(2):
         for q in range(2):
             cols = slice((h * 2 + q) * QW, (h * 2 + q + 1) * QW)
@@ -143,6 +155,7 @@
         return wrap(z + (4 - 2 * k - j if h == 0 else 2 * k + j - 3), NZ)
 
     def pack_cot():
+        icopies[1].wait()
         for k, nb in enumerate(group):
             arrived(cnts.at[0], m_s.at[k], m_r.at[k])
         total = jnp.sum(cnts[...], axis=0)[0:1]
@@ -280,65 +293,99 @@
             rps[0, pl.ds(chip, 1), :] = jnp.where(lane1 < 64, row, 0.0)
 
     def part(u, d):
-        if u == 2:
-            h = 0 if 1 <= d <= 4 else 1
-            i = 4 - d if h == 0 else d + 3
-            xs = cb[h, i // 2, :, i % 2].reshape(1024, ZW)
-        else:
-            d = wrap(z + d, NZ)
-            cols = pl.ds(pl.multiple_of(lax.rem(d, 2) * ZW, 128), ZW)
-            xs = tb[lax.div(d, 4), :, lax.rem(lax.div(d, 2), 2), :, cols].reshape(1024, ZW)
+        h = 0 if 1 <= d <= 4 else 1
+        i = 4 - d if h == 0 else d + 3
+        xs = cb[h, i // 2, :, i % 2].reshape(1024, ZW)
         return nn(dT[u * FH:(u + 1) * FH, :], xs)
 
-    units = (2, 0, 1)
     HF = FH // 2
     STEPS = NZ // 2
-
-    def z_unit(s, u):
+    OFFS = {k: (STEPS + 1 - k, k - STEPS - 1) for k in range(1, STEPS + 1)}
+    ways = ((0, zplus), (1, zminus))
+
+    def z_down(s):
         if s == 1:
-            val = part(u, STEPS).astype(BF16)
-            for dr, to in ((0, zplus), (1, zminus)):
-                zs[dr, 0, u, dr * HF:(dr + 1) * HF, :] = val[dr * HF:(dr + 1) * HF]
-                ref = (dr, 0, u, pl.ds(dr * HF, HF))
-                send(zs.at[ref], zr.at[ref], z_s.at[dr, 0, u], z_r.at[dr, 0, u], to)
-            return
-        for dr, to, off in ((0, zplus, STEPS + 1 - s), (1, zminus, s - STEPS - 1)):
-            val = part(u, off)
-            if s == 2:
-                ref = zr.at[dr, 0, u, pl.ds(dr * HF, HF)]
-                arrived(ref, z_s.at[dr, 0, u], z_r.at[dr, 0, u])
-                lo, hi = dr * HF, (dr + 1) * HF
-                o_lo, o_hi = HF - lo, FH - lo
-                zs[dr, 1, u, lo:hi, :] = (val[lo:hi] + ref[...].astype(F32)).astype(BF16)
-                zs[dr, 1, u, o_lo:o_hi, :] = val[o_lo:o_hi].astype(BF16)
+            val = part(2, STEPS).astype(BF16)
+        for dr, to in ways:
+            lo, hi = dr * HF, (dr + 1) * HF
+            sems = (z_s.at[dr, s - 1, 4], z_r.at[dr, s - 1, 4])
+            if s == 1:
+                zs[dr, 0, 2, lo:hi, :] = val[lo:hi]
+                ref = (dr, 0, 2, pl.ds(lo, HF))
             else:
-                ref = zr.at[dr, s - 2, u]
-                arrived(ref, z_s.at[dr, s - 2, u], z_r.at[dr, s - 2, u])
-                zs[dr, s - 1, u] = (val + ref[...].astype(F32)).astype(BF16)
-            send(zs.at[dr, s - 1, u], zr.at[dr, s - 1, u], z_s.at[dr, s - 1, u], z_r.at[dr, s - 1, u], to)
+                ref = (dr, s - 1, 2)
+                own = part(2, OFFS[s][dr])
+                if s == 2:
+                    got = zr.at[dr, 0, 2, pl.ds(lo, HF)]
+                    arrived(got, z_s.at[dr, 0, 4], z_r.at[dr, 0, 4])
+                    zs[dr, 1, 2, lo:hi, :] = (own[lo:hi] + got[...].astype(F32)).astype(BF16)
+                    zs[dr, 1, 2, HF - lo:FH - lo, :] = own[HF - lo:FH - lo].astype(BF16)
+                else:
+                    got = zr.at[dr, s - 2, 2]
+                    arrived(got, z_s.at[dr, s - 2, 4], z_r.at[dr, s - 2, 4])
+                    zs[dr, s - 1, 2] = (own + got[...].astype(F32)).astype(BF16)
+            send(zs.at[ref], zr.at[ref], *sems, to)
+
+    def gu_part(off):
+        d = wrap(z + off, NZ)
+        cols = pl.ds(pl.multiple_of(lax.rem(d, 2) * ZW, 128), ZW)
+        xs = tb[lax.div(d, 4), :, lax.rem(lax.div(d, 2), 2), :, cols].reshape(1024, ZW)
+        return nn(dT[0:2 * FH, :], xs)
+
+    def z_pre(s):
+        offs = (STEPS,) if s == 1 else (0,) if s > STEPS else OFFS[s]
+        for k, off in enumerate(offs):
+            pre[k * 512:(k + 1) * 512, 0:ZW] = gu_part(off)
+
+    def z_piece(s, k):
+        u, rows = k // 2, pl.ds(k % 2 * HF, HF)
+        for dr, to in ways:
+            if s == 1 and k % 2 != dr:
+                continue
+            base = 0 if s == 1 else dr * 512
+            val = pre[base + k * HF:base + (k + 1) * HF, 0:ZW]
+            if s > 2 or (s == 2 and k % 2 == dr):
+                got = zr.at[dr, s - 2, u, rows]
+                arrived(got, z_s.at[dr, s - 2, k], z_r.at[dr, s - 2, k])
+                val = val + got[...].astype(F32)
+            ref = (dr, s - 1, u, rows)
+            zs[ref] = val.astype(BF16)
+            send(zs.at[ref], zr.at[ref], z_s.at[dr, s - 1, k], z_r.at[dr, s - 1, k], to)
 
     def z_step(s):
-        for u in units:
-            z_unit(s, u)
-
-    outs = (gg_ref, gu_ref, gd_ref)
+        for k in range(4):
+            z_piece(s, k)
+
+    outs = (gg_hbm, gu_hbm, gd_hbm)
     mycols = pl.ds(pl.multiple_of(yh * FH, FH), FH)
     yourcols = pl.ds(pl.multiple_of((1 - yh) * FH, FH), FH)
-
-    def z_last(u):
-        val = part(u, 0)
+    myrows = pl.ds(pl.multiple_of(yh * 192, 192), 192)
+    yourrows = pl.ds(pl.multiple_of((1 - yh) * 192, 192), 192)
+
+    def z_last(k):
+        u, lo = k // 2, k % 2 * HF
+        if u == 2:
+            val = nn(dT[k * HF:(k + 1) * HF, :], cb[1, 1, :, 1].reshape(1024, ZW))
+        else:
+            val = pre[k * HF:(k + 1) * HF, 0:ZW]
         for dr in range(2):
-            ref = zr.at[dr, STEPS - 1, u]
-            arrived(ref, z_s.at[dr, STEPS - 1, u], z_r.at[dr, STEPS - 1, u])
-            val = val + ref[...].astype(F32)
-        fsum[u] = val.T
-        fxs[u] = fsum[u, pl.ds(pl.multiple_of((1 - yh) * 192, 192), 192), :].astype(BF16)
-        send(fxs.at[u], fxr.at[u], fx_s.at[u], fx_r.at[u], partner)
-        outs[u][:, mycols] = fsum[u, pl.ds(pl.multiple_of(yh * 192, 192), 192), :]
+            got = zr.at[dr, STEPS - 1, u, pl.ds(lo, HF)]
+            if u < 2:
+                arrived(got, z_s.at[dr, STEPS - 1, k], z_r.at[dr, STEPS - 1, k])
+            elif k == 4:
+                arrived(zr.at[dr, STEPS - 1, u], z_s.at[dr, STEPS - 1, 4], z_r.at[dr, STEPS - 1, 4])
+            val = val + got[...].astype(F32)
+        fsum[k] = val.T
+        fxs[k] = fsum[k, yourrows, :].astype(BF16)
+        send(fxs.at[k], fxr.at[k], fx_s.at[k], fx_r.at[k], partner)
+        wob[u, :, pl.ds(pl.multiple_of(yh * FH + lo, HF), HF)] = fsum[k, myrows, :]
 
     def z_out(u):
-        arrived(fxr.at[u], fx_s.at[u], fx_r.at[u])
-        outs[u][:, yourcols] = fxr[u].astype(F32)
+        for k in (2 * u, 2 * u + 1):
+            arrived(fxr.at[k], fx_s.at[k], fx_r.at[k])
+            at_ = pl.ds(pl.multiple_of((1 - yh) * FH + k % 2 * HF, HF), HF)
+            wob[u, :, at_] = fxr[k].astype(F32)
+        write(wob.at[u], outs[u], u)
 
     def wrows(h, q):
         return wgu[pl.ds(pl.multiple_of((h * 2 + q) * QW, QW), QW), :]
@@ -401,6 +448,7 @@
         for h in range(2):
             for q in range(2):
                 gt_ref[:, (h * 2 + q) * QW:(h * 2 + q + 1) * QW] = nn(place, fing[h, q]).astype(BF16)
+        write(gt_ref, gt_hbm, 3)
 
     def r_send(k):
         send(rps.at[k], rpr.at[k], rt_s.at[k], rt_r.at[k], hyper[k])
@@ -415,115 +463,125 @@
         lanes = (slot_r + (c * SL).astype(F32) == row_i.astype(F32)) & (routed_r > 0.5)
         summed = jnp.sum(jnp.where(lanes, column, 0.0), axis=0, keepdims=True)
         gr_ref[...] = jnp.where(routed > 0.5, summed / jnp.maximum(prob, 0.25), 0.0)
-
-    GATE, UP, DOWN = 0, 1, 2
+        write(gr_ref, gr_hbm, 4)
+
     swapped(0, tok_rows, 0)
     T[BEGIN]()
     pack_cot()
     swapped(1, cot_rows, 0)
     C1[BEGIN]()
     T[FIRST]()
+    T[SECOND]()
     T[NEAR](0)
-    T[SECOND]()
-    C1[FIRST]()
-    C1[NEAR](0)
     T[NEAR](1)
     T[NEAR](2)
-    T[FAR](0)
-    C1[SECOND]()
     T[NEAR](3)
     T[FAR](1)
+    C1[FIRST]()
+    T[FAR](0)
     T[FAR](2)
-    C2[BEGIN]()
-    C1[NEAR](1)
+    C1[NEAR](0)
     T[FAR](3)
     swapped(0, tok_rows, 1)
     T[FROM_SIB]()
     for cp in wcopies:
         cp.wait()
     fwd(0)
+    C1[SECOND]()
+    fwd(1)
+    C2[BEGIN]()
+    C1[NEAR](1)
+    fwd(2)
+    activate(0)
+    C1[NEAR](3)
     C1[NEAR](2)
+    fwd(3)
+    activate(1)
+    activate(2)
     C1[FAR](0)
-    fwd(1)
+    activate(3)
+    C1[FAR](1)
+    C1[FAR](2)
+    C1[FAR](3)
+    swapped(1, cot_rows, 1)
+    C1[FROM_SIB]()
+    z_down(1)
     C2[FIRST]()
     C2[NEAR](0)
-    fwd(2)
-    C1[NEAR](3)
-    C1[FAR](1)
-    C1[FAR](2)
-    fwd(3)
+    back_part(0, 1)
     C2[SECOND]()
-    activate(0)
-    activate(1)
-    C1[FAR](3)
+    z_down(2)
+    back_part(0, 0)
     C2[NEAR](1)
+    back_part(0, 2)
     C2[NEAR](2)
-    activate(2)
-    activate(3)
+    C2[NEAR](3)
+    back_part(0, 3)
     C2[FAR](0)
-    swapped(1, cot_rows, 1)
-    C1[FROM_SIB]()
-    z_unit(1, DOWN)
-    C2[NEAR](3)
-    for i in range(4):
-        back_part(0, i)
     C2[FAR](1)
     C2[FAR](2)
-    z_unit(2, DOWN)
     C2[FAR](3)
     C2[FROM_SIB]()
-    z_unit(3, DOWN)
+    z_down(3)
     for i in range(4):
         back_part(1, i)
         gradients(2 * i)
         gradients(2 * i + 1)
-    z_unit(1, GATE)
-    z_unit(1, UP)
+    z_pre(1)
+    z_step(1)
     r_send(0)
     g_sib(0)
     g1()
-    z_unit(4, DOWN)
-    g_sib(1)
+    z_down(4)
+    z_pre(2)
     r_got(0)
     r_send(1)
-    z_unit(2, GATE)
+    g_sib(1)
+    z_step(2)
     g_sib(2)
-    z_unit(2, UP)
+    g_sib(3)
+    z_pre(3)
     r_got(1)
     r_send(2)
     g_2(0)
     g_2(1)
-    g_sib(3)
-    z_unit(3, GATE)
+    z_step(3)
+    z_pre(4)
     r_got(2)
     r_send(3)
+    z_last(4)
+    z_last(5)
     g3()
-    z_unit(3, UP)
-    z_last(DOWN)
+    z_step(4)
+    z_pre(5)
     r_got(3)
     r_send(4)
     g4()
-    z_unit(4, GATE)
+    z_out(2)
     r_got(4)
     r_out()
     g5()
-    z_unit(4, UP)
-    z_out(DOWN)
     g6()
-    z_last(GATE)
-    z_last(UP)
-    z_out(GATE)
-    z_out(UP)
+    for k in range(4):
+        z_last(k)
+    z_out(0)
+    z_out(1)
+    for cp in written:
+        cp.wait()
     for cp in sent:
         cp.wait_send()
 
 
 def copies(*refs):
-    ins, outs, sem = refs[:5], refs[5:10], refs[10]
-    moves = [pltpu.make_async_copy(a, b, sem.at[k]) for k, (a, b) in enumerate(zip(ins, outs))]
-    for cp in moves:
+    ins, outs, held, sem = refs[:5], refs[5:10], refs[10:15], refs[15]
+    reads = [pltpu.make_async_copy(a, h, sem.at[0, k]) for k, (a, h) in enumerate(zip(ins, held))]
+    writes = [pltpu.make_async_copy(h, b, sem.at[1, k]) for k, (h, b) in enumerate(zip(held, outs))]
+    for cp in reads:
         cp.start()
-    for cp in moves:
+    for read, write in zip(reads, writes):
+        read.wait()
+        write.start()
+    for cp in writes:
         cp.wait()
 
 
@@ -534,7 +592,7 @@
         out_shape=tuple(jax.ShapeDtypeStruct(a.shape, a.dtype) for a in arrays),
         in_specs=[hbm] * 5,
         out_specs=(hbm,) * 5,
-        scratch_shapes=[pltpu.SemaphoreType.DMA((5,))],
+        scratch_shapes=[pltpu.VMEM(a.shape, a.dtype) for a in arrays] + [pltpu.SemaphoreType.DMA((2, 5))],
         compiler_params=pltpu.CompilerParams(vmem_limit_bytes=62 * 1024 * 1024),
     )(*arrays)
 
@@ -547,6 +605,11 @@
     d = tokens.shape[2]
     dma = pltpu.SemaphoreType.DMA
     scratch = [
+        pltpu.VMEM((128, d), BF16),
+        pltpu.VMEM((128, d), BF16),
+        pltpu.VMEM((128, d), BF16),
+        pltpu.VMEM((1, 128), F32),
+        pltpu.VMEM((3, 192, 2 * FH), F32),
         pltpu.VMEM((2, 16, 2, 64, QW), BF16),
         pltpu.VMEM((2, 2, 16, 2, 64, ZW), BF16),
         pltpu.VMEM((16, 8, 128), F32),
@@ -574,32 +637,34 @@
         pltpu.VMEM((2, 2, SL, QW), BF16),
         pltpu.VMEM((6, 16, 128), F32),
         pltpu.VMEM((5, 16, 128), F32),
-        pltpu.VMEM((3, ZW, FH), F32),
-        pltpu.VMEM((3, 192, FH), BF16),
-        pltpu.VMEM((3, 192, FH), BF16),
+        pltpu.VMEM((6, ZW, FH // 2), F32),
+        pltpu.VMEM((6, 192, FH // 2), BF16),
+        pltpu.VMEM((6, 192, FH // 2), BF16),
+        dma((2,)),
+        dma((5,)),
         dma((3,)),
         dma((3, 20)), dma((3, 20)),
         dma((3, 15)), dma((3, 15)),
         dma((2, 2)), dma((2, 2)),
         dma((15,)), dma((15,)),
-        dma((2, NZ // 2, 3)), dma((2, NZ // 2, 3)),
+        dma((2, NZ // 2, 5)), dma((2, NZ // 2, 5)),
         dma((13,)), dma((13,)),
         dma((5,)), dma((5,)),
-        dma((3,)), dma((3,)),
+        dma((6,)), dma((6,)),
     ]
     shape = jax.ShapeDtypeStruct
     grads = shape((192, 2 * FH), F32)
     gt, gr, gg, gu, gd = pl.pallas_call(
         kernel,
         out_shape=(shape((128, d), BF16), shape((1, 128), F32), grads, grads, grads),
-        in_specs=[vmem] * 5 + [hbm] * 3,
-        out_specs=(vmem,) * 5,
+        in_specs=[vmem] * 3 + [hbm] * 5,
+        out_specs=(hbm,) * 5,
         scratch_shapes=scratch,
         compiler_params=pltpu.CompilerParams(
             collective_id=0, has_side_effects=True, vmem_limit_bytes=62 * 1024 * 1024),
         cost_estimate=pl.CostEstimate(
             flops=13 * 10**9, bytes_accessed=14 * 10**6, transcendentals=1024 * FH),
-    )(tokens[0], cotangent[0], route_ids[0].T, route_weight[0].T, segment_ids,
+    )(route_ids[0].T, route_weight[0].T, segment_ids, tokens[0], cotangent[0],
       gate_weight, up_weight, down_weight)
     gt, gr, gg, gu, gd = hand_over(gt, gr, gg, gu, gd)
     return gt[None], gr, gg, gu, gd

time: 172 us -> 112 us (0.65)
  Pallas kernels: 171 us -> 112 us
    pallas_call x1, Pallas kernels: 60.7 us -> 2.49 us  [hand_over(): pl.pallas_call(copies, out_shape=tuple((jax.ShapeDtypeStruct(a.shape, a.d...]
where the time goes in v3:
time: 112 us
  Pallas kernels  112 us (100%)
    pallas_call x1, Pallas kernels, shards(): pl.pallas_call(kernel, out_shape=(shape((128, d), BF16), shape((1, 128),...  109 us
    pallas_call x1, Pallas kernels, hand_over(): pl.pallas_call(copies, out_shape=tuple((jax.ShapeDtypeStruct(a.shape, a.d...  2.49 us

profile of v3, /device:TPU:1, one launch (start us, length us, event | category | flops | bytes accessed | tf_op | source)
XLA Modules:
  0.0 112.3 jit_solution(10018589035460804276)
XLA Ops:
  0.6 109.0 %shard_map.119 = (bf16[128,3072]{1,0:T(8,128)(2,1)}, f32[1,128]{1,0:T(1,128)}, f32[192,512]{1,0:T(8,128)}, f32[192,512]{1,0:T(8,128)}, f32[192,512]{1,0:T(8,128)}) custom-call(s32[2,128]{1,0:T(2,128)} %bitcast.12, bf16[2,128]{1,0:T(2,128)(2,1)} %bitcast.13, s32[1,128]{1,0:T(1,128)} %seg_ref.1, bf16[128,3072]{1,0:T(8,128)(2,1)} %bitcast.9, ...), custom_call_target="tpu_custom_call" | custom-call | flops 12999999488 | bytes 14000000 | tf_op jit(solution)/shard_map/pallas_call | solution.py:657
  109.7 2.5 %shard_map.120 = (bf16[128,3072]{1,0:T(8,128)(2,1)}, f32[1,128]{1,0:T(1,128)}, f32[192,512]{1,0:T(8,128)}, f32[192,512]{1,0:T(8,128)}, f32[192,512]{1,0:T(8,128)}) custom-call(bf16[128,3072]{1,0:T(8,128)(2,1)} %get-tuple-element.15.refs_0_, f32[1,128]{1,0:T(1,128)} %get-tuple-element.16.refs_1_, f32[192,512]{1,0:T(8,128)} %get-tuple-element.17.refs_2_, ...), custom_call_target="tpu_custom_call" | custom-call | tf_op jit(solution)/shard_map/pallas_call | solution.py:590

commit v4 on v3

--- a/solution.py
+++ b/solution.py
@@ -13,6 +13,7 @@
 ZW = 384
 FH = 256
 SL = 32
+FAR_FIRST = ((4, 3, -3, 2), (-2, 1, -1, 0))
 
 
 def nn(a, b):
@@ -30,10 +31,10 @@
 def kernel(
     ids_ref, rw_ref, seg_ref, tok_hbm, cot_hbm, wg_hbm, wu_hbm, wd_hbm,
     gt_hbm, gr_hbm, gg_hbm, gu_hbm, gd_hbm,
-    tok_ref, cot_ref, gt_ref, gr_ref, wob,
+    tok_ref, cot_ref, picked, gt_ref, gr_ref, wob,
     tb, cb, cnts, wgu, wd, pre, hidb, backb, dgu, dT, zs, zr, sgs, sgr, p1s, p1r, p2s, p2r, g2,
     q1s, q1r, q2s, q2r, fin, fing, rps, rpr, fsum, fxs, fxr,
-    i_sem, o_sem, w_sem, ag_s, ag_r, sib_s, sib_r, sw_s, sw_r, m_s, m_r, z_s, z_r, g_s, g_r, rt_s, rt_r, fx_s, fx_r,
+    i_sem, o_sem, w_sem, ag_s, ag_r, sib_s, sib_r, m_s, m_r, z_s, z_r, g_s, g_r, rt_s, rt_r, fx_s, fx_r,
 ):
     dp, et = lax.axis_index("dp"), lax.axis_index("et")
     z, yh = lax.div(dp, 2), lax.rem(dp, 2)
@@ -122,58 +123,38 @@
     mine = pl.ds(pl.multiple_of(c * SL, SL), SL)
     other = pl.ds(pl.multiple_of((1 - c) * SL, SL), SL)
     here = p * 4 + r
-    there = r * 4 + p
 
     icopies[0].wait()
-    for h in range(2):
-        for q in range(2):
-            cols = slice((h * 2 + q) * QW, (h * 2 + q + 1) * QW)
-            tb[h, here, q, mine, :] = nn(pick, tok_ref[:, cols]).astype(BF16)
+    for q in range(4):
+        tb[c, here, q] = nn(pick, tok_ref[:, q * QW:(q + 1) * QW]).astype(BF16)
+    icopies[1].wait()
+    for q in range(4):
+        picked[:, q * QW:(q + 1) * QW] = nn(pick, cot_ref[:, q * QW:(q + 1) * QW]).astype(BF16)
+    slot_member = nt(pick, member)
+    slot_prob = jnp.sum(nt(pick, jnp.where(row_i == 16, prob, 0.0).astype(BF16)), axis=1, keepdims=True)
 
     pl.semaphore_wait(barrier, len(group) + 4)
-    for k, nb in enumerate(group):
-        send(cnts.at[et], cnts.at[et], m_s.at[k], m_r.at[k], nb)
-
-    def tok_rows(h, rows):
-        return tb.at[h, here, :, rows, :], tb.at[h, there, :, rows, :]
-
-    def cot_rows(h, rows):
-        return cb.at[h, :, here, :, rows, :], cb.at[h, :, there, :, rows, :]
-
-    def swap(t, rows_of):
-        for k, h in ((0, 1 - c), (1, c)):
-            src, dst = rows_of(h, mine)
-            send(src, dst, sw_s.at[t, k], sw_r.at[t, k], sib)
-
-    def swapped(t, rows_of, k):
-        h = c if k == 0 else 1 - c
-        arrived(rows_of(h, other)[0], sw_s.at[t, k], sw_r.at[t, k])
-
-    swap(0, tok_rows)
-
-    def far_first(h, k, j):
-        return wrap(z + (4 - 2 * k - j if h == 0 else 2 * k + j - 3), NZ)
-
-    def pack_cot():
-        icopies[1].wait()
+
+    def send_counts():
         for k, nb in enumerate(group):
-            arrived(cnts.at[0], m_s.at[k], m_r.at[k])
+            send(cnts.at[et], cnts.at[et], m_s.at[k], m_r.at[k], nb)
+
+    def pack_cot(i):
+        if i == 0:
+            for k, nb in enumerate(group):
+                arrived(cnts.at[0], m_s.at[k], m_r.at[k])
         total = jnp.sum(cnts[...], axis=0)[0:1]
-        slot_count = jnp.sum(nt(pick, member) * total, axis=1, keepdims=True)
-        slot_prob = jnp.sum(nt(pick, jnp.where(row_i == 16, prob, 0.0).astype(BF16)), axis=1, keepdims=True)
+        slot_count = jnp.sum(slot_member * total, axis=1, keepdims=True)
         scale = jnp.where(slot_count > 0.0, slot_prob / jnp.maximum(slot_count, 1.0), 0.0)
-        for h in range(2):
-            for k in range(2):
-                for j in range(2):
-                    cols = pl.ds(pl.multiple_of(far_first(h, k, j) * ZW, 128), ZW)
-                    cb[h, k, here, j, mine, :] = (nn(pick, cot_ref[:, cols]) * scale).astype(BF16)
-        swap(1, cot_rows)
+        for j in range(4):
+            cols = pl.ds(pl.multiple_of(wrap(z + FAR_FIRST[i][j], NZ) * ZW, 128), ZW)
+            cb[i, c, here, j] = (picked[:, cols].astype(F32) * scale).astype(BF16)
 
     line = (0, -1, 1, 2)
 
     def ag(t, at_core):
         def ref_of(h, place_, q):
-            return at_core(h, place_) if q is None else at_core(h, place_).at[q]
+            return at_core(h, place_) if q is None else at_core(h, place_, q)
 
         def one(dst_p, dst_r, q, k, to):
             ref = ref_of(c, pos(dst_p, dst_r), q)
@@ -183,7 +164,7 @@
             arrived(ref_of(c, pos(dst_p, dst_r), q), ag_s.at[t, k], ag_r.at[t, k])
 
         def to_sib(a, b):
-            k = (a % 4) * 4 + b % 4 - 1
+            k = (a % 4) * 4 + b % 4
             send(at_core(c, pos(a, b)), at_core(c, wrap(r + b, 4) * 4 + wrap(p + a, 4)),
                  sib_s.at[t, k], sib_r.at[t, k], sib)
 
@@ -195,6 +176,7 @@
             one(0, 0, None, 0, at(0, 1))
             one(0, 0, None, 1, at(0, -1))
             out_p(0)
+            to_sib(0, 0)
 
         def first():
             got(0, -1, None, 0)
@@ -228,47 +210,48 @@
         def from_sib():
             for a in range(4):
                 for b in range(4):
-                    if a or b:
-                        k = a * 4 + b - 1
-                        arrived(at_core(1 - c, pos(b, a)), sib_s.at[t, k], sib_r.at[t, k])
+                    k = a * 4 + b
+                    arrived(at_core(1 - c, pos(b, a)), sib_s.at[t, k], sib_r.at[t, k])
 
         return begin, first, second, near, far, from_sib
 
-    T = ag(0, lambda h, i: tb.at[h, i])
-    C1 = ag(1, lambda h, i: cb.at[h, 0, i])
-    C2 = ag(2, lambda h, i: cb.at[h, 1, i])
+    def tok_at(h, i, q=None):
+        return tb.at[h, i] if q is None else tb.at[h, i, pl.ds(2 * q, 2)]
+
+    def cot_at(k):
+        return lambda h, i, q=None: cb.at[k, h, i] if q is None else cb.at[k, h, i, pl.ds(2 * q, 2)]
+
+    T, C1, C2 = ag(0, tok_at), ag(1, cot_at(0)), ag(2, cot_at(1))
     BEGIN, FIRST, SECOND, NEAR, FAR, FROM_SIB = range(6)
 
     def fwd(i):
         rows = pl.ds(pl.multiple_of(i * 256, 256), 256)
         acc = None
-        for h in range(2):
-            for q in range(2):
-                xs = tb[h, pl.ds(i * 4, 4), q].reshape(256, QW)
-                one = nn(xs, wgu[(h * 2 + q) * QW:(h * 2 + q + 1) * QW, :])
-                acc = one if acc is None else acc + one
+        for q in range(4):
+            xs = tb[i // 2, pl.ds(i % 2 * 8, 8), q].reshape(256, QW)
+            one = nn(xs, wgu[q * QW:(q + 1) * QW, :])
+            acc = one if acc is None else acc + one
         pre[rows, :] = acc
 
     def activate(i):
         for j in (2 * i, 2 * i + 1):
             rows = pl.ds(j * n, n)
             gate, up = pre[rows, 0:FH], pre[rows, FH:2 * FH]
-            sg = 1.0 / (1.0 + jnp.exp(-gate))
+            sg = 0.5 * jnp.tanh(0.5 * gate) + 0.5
             act = gate * sg
             hid = act * up
             pre[rows, 0:FH] = up * (sg * (1.0 + gate * (1.0 - sg)))
             pre[rows, FH:2 * FH] = act
             hidb[rows, :] = hid
-            dT[2 * FH:3 * FH, rows] = hid.T.astype(BF16)
+            dT[2 * FH:3 * FH, rows] = hid.astype(BF16).T
 
     def back_part(k, i):
         rows = pl.ds(i * 256, 256)
         acc = None
-        for h in range(2):
-            for j in range(2):
-                xs = cb[h, k, pl.ds(i * 4, 4), j].reshape(256, ZW)
-                one = nn(xs, wd[pl.ds(pl.multiple_of(far_first(h, k, j) * ZW, ZW), ZW), :])
-                acc = one if acc is None else acc + one
+        for j in range(4):
+            xs = cb[k, i // 2, pl.ds(i % 2 * 8, 8), j].reshape(256, ZW)
+            one = nn(xs, wd[pl.ds(pl.multiple_of(wrap(z + FAR_FIRST[k][j], NZ) * ZW, ZW), ZW), :])
+            acc = one if acc is None else acc + one
         if k == 0:
             backb[rows, :] = acc
         else:
@@ -280,28 +263,38 @@
         rows = pl.ds(j * n, n)
         back = backb[rows, :]
         dg, du = back * pre[rows, 0:FH], back * pre[rows, FH:2 * FH]
-        dgu[j // 2, j % 2, :, 0:FH] = dg.astype(BF16)
-        dgu[j // 2, j % 2, :, FH:2 * FH] = du.astype(BF16)
-        dT[0:FH, rows] = dg.T.astype(BF16)
-        dT[FH:2 * FH, rows] = du.T.astype(BF16)
-        rp = jnp.sum(hidb[rows, :] * back, axis=1, keepdims=True)
+        dg, du = dg.astype(BF16), du.astype(BF16)
+        dgu[j // 4, j % 4, :, :, 0:FH] = dg.reshape(4, SL, FH)
+        dgu[j // 4, j % 4, :, :, FH:2 * FH] = du.reshape(4, SL, FH)
+        dT[0:FH, rows] = dg.T
+        dT[FH:2 * FH, rows] = du.T
+
+    def route_part(j):
+        rows = pl.ds(j * n, n)
+        rp = jnp.sum(hidb[rows, :] * backb[rows, :], axis=1, keepdims=True)
         rp_row = jnp.broadcast_to(rp, (n, n)).T[0:1]
-        for k in range(2):
-            i = j * 2 + k
-            chip = i + c * (i % 4 * 4 + i // 4 - i)
-            row = rp_row if k == 0 else pltpu.roll(rp_row, 64, 1)
-            rps[0, pl.ds(chip, 1), :] = jnp.where(lane1 < 64, row, 0.0)
+        k, pp = j // 4, j % 4
+        for rr in range(4):
+            chip = pp * 4 + rr + c * (rr * 4 + pp - pp * 4 - rr)
+            shift = (k * SL - rr * SL) % n
+            row = rp_row if shift == 0 else pltpu.roll(rp_row, shift, 1)
+            row = jnp.where((lane1 >= k * SL) & (lane1 < (k + 1) * SL), row, 0.0)
+            if k == 0:
+                rps[0, pl.ds(chip, 1), :] = row
+            else:
+                rps[0, pl.ds(chip, 1), :] += row
 
     def part(u, d):
-        h = 0 if 1 <= d <= 4 else 1
-        i = 4 - d if h == 0 else d + 3
-        xs = cb[h, i // 2, :, i % 2].reshape(1024, ZW)
+        k = 0 if d in FAR_FIRST[0] else 1
+        xs = cb[k, :, :, FAR_FIRST[k].index(d)].reshape(1024, ZW)
         return nn(dT[u * FH:(u + 1) * FH, :], xs)
 
     HF = FH // 2
     STEPS = NZ // 2
     OFFS = {k: (STEPS + 1 - k, k - STEPS - 1) for k in range(1, STEPS + 1)}
     ways = ((0, zplus), (1, zminus))
+    myrows = pl.ds(pl.multiple_of(yh * 192, 192), 192)
+    yourrows = pl.ds(pl.multiple_of((1 - yh) * 192, 192), 192)
 
     def z_down(s):
         if s == 1:
@@ -329,7 +322,7 @@
     def gu_part(off):
         d = wrap(z + off, NZ)
         cols = pl.ds(pl.multiple_of(lax.rem(d, 2) * ZW, 128), ZW)
-        xs = tb[lax.div(d, 4), :, lax.rem(lax.div(d, 2), 2), :, cols].reshape(1024, ZW)
+        xs = tb[:, :, lax.div(d, 2), :, cols].reshape(1024, ZW)
         return nn(dT[0:2 * FH, :], xs)
 
     def z_pre(s):
@@ -357,15 +350,12 @@
             z_piece(s, k)
 
     outs = (gg_hbm, gu_hbm, gd_hbm)
-    mycols = pl.ds(pl.multiple_of(yh * FH, FH), FH)
-    yourcols = pl.ds(pl.multiple_of((1 - yh) * FH, FH), FH)
-    myrows = pl.ds(pl.multiple_of(yh * 192, 192), 192)
-    yourrows = pl.ds(pl.multiple_of((1 - yh) * 192, 192), 192)
 
     def z_last(k):
         u, lo = k // 2, k % 2 * HF
         if u == 2:
-            val = nn(dT[k * HF:(k + 1) * HF, :], cb[1, 1, :, 1].reshape(1024, ZW))
+            xs = cb[1, :, :, FAR_FIRST[1].index(0)].reshape(1024, ZW)
+            val = nn(dT[k * HF:(k + 1) * HF, :], xs)
         else:
             val = pre[k * HF:(k + 1) * HF, 0:ZW]
         for dr in range(2):
@@ -380,29 +370,34 @@
         send(fxs.at[k], fxr.at[k], fx_s.at[k], fx_r.at[k], partner)
         wob[u, :, pl.ds(pl.multiple_of(yh * FH + lo, HF), HF)] = fsum[k, myrows, :]
 
-    def z_out(u):
-        for k in (2 * u, 2 * u + 1):
-            arrived(fxr.at[k], fx_s.at[k], fx_r.at[k])
-            at_ = pl.ds(pl.multiple_of((1 - yh) * FH + k % 2 * HF, HF), HF)
-            wob[u, :, at_] = fxr[k].astype(F32)
-        write(wob.at[u], outs[u], u)
+    def z_out(k):
+        u, lo = k // 2, k % 2 * HF
+        arrived(fxr.at[k], fx_s.at[k], fx_r.at[k])
+        wob[u, :, pl.ds(pl.multiple_of((1 - yh) * FH + lo, HF), HF)] = fxr[k].astype(F32)
+        if k % 2:
+            write(wob.at[u], outs[u], u)
 
     def wrows(h, q):
         return wgu[pl.ds(pl.multiple_of((h * 2 + q) * QW, QW), QW), :]
 
     def g_sib(k):
         rr = wrap(r + (2, 1, -1, 0)[k], 4)
-        j0, odd = lax.div(rr, 2), lax.rem(rr, 2)
-        xs = dgu[:, j0, pl.ds(pl.multiple_of(odd * 64, 64), 64), :].reshape(256, 2 * FH)
-        for q in range(2):
-            sgs[rr, :, q] = nt(xs, wrows(1 - c, q)).astype(BF16).reshape(4, 64, QW)
+        xs = dgu[:, :, rr].reshape(256, 2 * FH)
+        for q in range(2):
+            val = nt(xs, wrows(1 - c, q)).astype(BF16).reshape(2, 4, SL, QW)
+            for k2 in range(2):
+                sgs[rr, :, q, k2 * SL:(k2 + 1) * SL, :] = val[k2]
         send(sgs.at[rr], sgr.at[rr], g_s.at[k], g_r.at[k], sib)
 
     def g_line(off, k):
         pp = wrap(p + off, 4)
         arrived(sgr.at[pp], g_s.at[k], g_r.at[k])
-        xs = dgu[pp].reshape(256, 2 * FH)
-        return [nt(xs, wrows(c, q)).reshape(4, 64, QW) + sgr[pp, :, q].astype(F32) for q in range(2)]
+        xs = dgu[:, pp].reshape(256, 2 * FH)
+        out = []
+        for q in range(2):
+            val = nt(xs, wrows(c, q)).reshape(2, 4, SL, QW)
+            out.append(jnp.concatenate([val[0], val[1]], axis=1) + sgr[pp, :, q].astype(F32))
+        return out
 
     def g1():
         val = g_line(2, 0)
@@ -465,86 +460,86 @@
         gr_ref[...] = jnp.where(routed > 0.5, summed / jnp.maximum(prob, 0.25), 0.0)
         write(gr_ref, gr_hbm, 4)
 
-    swapped(0, tok_rows, 0)
     T[BEGIN]()
-    pack_cot()
-    swapped(1, cot_rows, 0)
+    send_counts()
+    pack_cot(0)
     C1[BEGIN]()
     T[FIRST]()
+    T[NEAR](0)
     T[SECOND]()
-    T[NEAR](0)
     T[NEAR](1)
     T[NEAR](2)
     T[NEAR](3)
+    pack_cot(1)
+    C2[BEGIN]()
+    T[FAR](0)
+    C1[FIRST]()
+    C1[NEAR](0)
     T[FAR](1)
-    C1[FIRST]()
-    T[FAR](0)
     T[FAR](2)
-    C1[NEAR](0)
+    C1[SECOND]()
     T[FAR](3)
-    swapped(0, tok_rows, 1)
     T[FROM_SIB]()
     for cp in wcopies:
         cp.wait()
+    C1[NEAR](1)
+    C1[NEAR](2)
     fwd(0)
-    C1[SECOND]()
+    C1[NEAR](3)
+    C2[FIRST]()
+    C2[NEAR](0)
     fwd(1)
-    C2[BEGIN]()
-    C1[NEAR](1)
+    C1[FAR](0)
+    C1[FAR](1)
     fwd(2)
+    C1[FAR](2)
+    C2[SECOND]()
+    fwd(3)
+    C1[FAR](3)
     activate(0)
-    C1[NEAR](3)
-    C1[NEAR](2)
-    fwd(3)
     activate(1)
+    C2[NEAR](1)
+    C2[NEAR](2)
     activate(2)
-    C1[FAR](0)
     activate(3)
-    C1[FAR](1)
-    C1[FAR](2)
-    C1[FAR](3)
-    swapped(1, cot_rows, 1)
     C1[FROM_SIB]()
     z_down(1)
-    C2[FIRST]()
-    C2[NEAR](0)
+    C2[NEAR](3)
+    back_part(0, 0)
     back_part(0, 1)
-    C2[SECOND]()
+    C2[FAR](0)
+    back_part(0, 2)
+    back_part(0, 3)
     z_down(2)
-    back_part(0, 0)
-    C2[NEAR](1)
-    back_part(0, 2)
-    C2[NEAR](2)
-    C2[NEAR](3)
-    back_part(0, 3)
-    C2[FAR](0)
     C2[FAR](1)
     C2[FAR](2)
     C2[FAR](3)
     C2[FROM_SIB]()
-    z_down(3)
     for i in range(4):
         back_part(1, i)
         gradients(2 * i)
         gradients(2 * i + 1)
     z_pre(1)
     z_step(1)
-    r_send(0)
     g_sib(0)
+    z_down(3)
     g1()
-    z_down(4)
     z_pre(2)
-    r_got(0)
-    r_send(1)
     g_sib(1)
     z_step(2)
+    for j in range(8):
+        route_part(j)
+    r_send(0)
+    z_down(4)
     g_sib(2)
     g_sib(3)
     z_pre(3)
+    r_got(0)
+    r_send(1)
+    g_2(0)
+    g_2(1)
     r_got(1)
     r_send(2)
-    g_2(0)
-    g_2(1)
     z_step(3)
     z_pre(4)
     r_got(2)
@@ -557,15 +552,16 @@
     r_got(3)
     r_send(4)
     g4()
-    z_out(2)
+    z_out(4)
+    z_out(5)
     r_got(4)
     r_out()
     g5()
     g6()
     for k in range(4):
         z_last(k)
-    z_out(0)
-    z_out(1)
+    for k in range(4):
+        z_out(k)
     for cp in written:
         cp.wait()
     for cp in sent:
@@ -607,18 +603,19 @@
     scratch = [
         pltpu.VMEM((128, d), BF16),
         pltpu.VMEM((128, d), BF16),
+        pltpu.VMEM((SL, d), BF16),
         pltpu.VMEM((128, d), BF16),
         pltpu.VMEM((1, 128), F32),
         pltpu.VMEM((3, 192, 2 * FH), F32),
-        pltpu.VMEM((2, 16, 2, 64, QW), BF16),
-        pltpu.VMEM((2, 2, 16, 2, 64, ZW), BF16),
+        pltpu.VMEM((2, 16, 4, SL, QW), BF16),
+        pltpu.VMEM((2, 2, 16, 4, SL, ZW), BF16),
         pltpu.VMEM((16, 8, 128), F32),
         pltpu.VMEM((d, 2 * FH), BF16),
         pltpu.VMEM((d, FH), BF16),
         pltpu.VMEM((1024, 2 * FH), F32),
         pltpu.VMEM((1024, FH), F32),
         pltpu.VMEM((1024, FH), F32),
-        pltpu.VMEM((4, 2, 128, 2 * FH), BF16),
+        pltpu.VMEM((2, 4, 4, SL, 2 * FH), BF16),
         pltpu.VMEM((3 * FH, 1024), BF16),
         pltpu.VMEM((2, NZ // 2, 3, FH, ZW), BF16),
         pltpu.VMEM((2, NZ // 2, 3, FH, ZW), BF16),
@@ -644,8 +641,7 @@
         dma((5,)),
         dma((3,)),
         dma((3, 20)), dma((3, 20)),
-        dma((3, 15)), dma((3, 15)),
-        dma((2, 2)), dma((2, 2)),
+        dma((3, 16)), dma((3, 16)),
         dma((15,)), dma((15,)),
         dma((2, NZ // 2, 5)), dma((2, NZ // 2, 5)),
         dma((13,)), dma((13,)),

time: 112 us -> 110 us (0.982); the launches traced: 112 us -> 109 us
  Pallas kernels: 112 us -> 108 us
    pallas_call x1, Pallas kernels: 109 us -> 105 us  [shards(): pl.pallas_call(kernel, out_shape=(shape((128, d), BF16), shape((1, 128),...]
where the time goes in v4:
time: 110 us; the launch traced here: 109 us
  Pallas kernels  108 us (98%)
    pallas_call x1, Pallas kernels, shards(): pl.pallas_call(kernel, out_shape=(shape((128, d), BF16), shape((1, 128),...  105 us
    pallas_call x1, Pallas kernels, hand_over(): pl.pallas_call(copies, out_shape=tuple((jax.ShapeDtypeStruct(a.shape, a.d...  2.49 us

profile of v4, /device:TPU:1, one launch (start us, length us, event | category | flops | bytes accessed | tf_op | source)
XLA Modules:
  0.0 108.8 jit_solution(17361603021732056234)
XLA Ops:
  0.6 105.5 %shard_map.119 = (bf16[128,3072]{1,0:T(8,128)(2,1)}, f32[1,128]{1,0:T(1,128)}, f32[192,512]{1,0:T(8,128)}, f32[192,512]{1,0:T(8,128)}, f32[192,512]{1,0:T(8,128)}) custom-call(s32[2,128]{1,0:T(2,128)} %bitcast.12, bf16[2,128]{1,0:T(2,128)(2,1)} %bitcast.13, s32[1,128]{1,0:T(1,128)} %seg_ref.1, bf16[128,3072]{1,0:T(8,128)(2,1)} %bitcast.9, ...), custom_call_target="tpu_custom_call" | custom-call | flops 12999999488 | bytes 14000000 | tf_op jit(solution)/shard_map/pallas_call | solution.py:653
  106.1 2.5 %shard_map.120 = (bf16[128,3072]{1,0:T(8,128)(2,1)}, f32[1,128]{1,0:T(1,128)}, f32[192,512]{1,0:T(8,128)}, f32[192,512]{1,0:T(8,128)}, f32[192,512]{1,0:T(8,128)}) custom-call(bf16[128,3072]{1,0:T(8,128)(2,1)} %get-tuple-element.15.refs_0_, f32[1,128]{1,0:T(1,128)} %get-tuple-element.16.refs_1_, f32[192,512]{1,0:T(8,128)} %get-tuple-element.17.refs_2_, ...), custom_call_target="tpu_custom_call" | custom-call | tf_op jit(solution)/shard_map/pallas_call | solution.py:586
